TPU v7x, 512 devices: a whole 4x8x8 slice. The times are simulated.
512 devices in a mesh: rep: 8 (over z_hi, core), fsdp: 16 (over y, z_lo), tp: 4 (over x).
Axes of the slice: x: 4, y: 8, z: 8 (z_hi: 4, z_lo: 2; z = z_hi * 2 + z_lo), core: 2. Of those that a mesh axis runs over, the one named last changes fastest.
Arguments:
- tokens: bfloat16 [32768, 8192], P(('rep', 'fsdp'), 'tp'), may hold values from -6 to 6
- cotangent: bfloat16 [32768, 1024], P(('rep', 'fsdp')), may hold values from -6 to 6
- codes: bfloat16 [8192, 1024], P('tp', 'fsdp'), may hold values from -384 to 384
- scales: bfloat16 [64, 1024], P('tp', 'fsdp'), may hold values from 8.6307526e-05 to 0.0003452301
- adapter_down: float32 [8192, 64], P('tp'), may hold values from -6 to 6
- adapter_up: float32 [64, 1024], replicated, may hold values from -6 to 6
Outputs:
- values: bfloat16 [32768, 1024], P(('rep', 'fsdp'), 'tp')
- grad_tokens: bfloat16 [32768, 8192], P(('rep', 'fsdp'), 'tp')
- refreshed_down: float32 [8192, 64], P('tp')
- scorer_a: bfloat16 [8192, 64], replicated
- refreshed_up: float32 [64, 1024], P(None, 'tp')
All inputs are finite; a program needn't handle non-finite values.
Results may differ from a plain program's by a relative error of at most 0.0053.
Values may be sent and summed in bfloat16 or wider, within the bound.
No kernel may reach another device: no remote copies, remote signals or barrier semaphores. Data moves between devices by JAX's collectives and lax.ppermute only.
A program may use at most 64 MiB of HBM per device.

v0:
```python
import math

import jax
import jax.numpy as jnp
from jax import lax
from jax.sharding import PartitionSpec as P

MODEL_WIDTH = 8192


adapter_scale = 0.25
down_learning_rate = 1.0
up_learning_rate = 0.1
eps_norm = 1e-06


def norm_divided(grad, axis):
    return grad * lax.rsqrt(jnp.mean(grad * grad, axis=axis, keepdims=True) + eps_norm)


def dequant(code_piece, scale_piece):
    block_count = scale_piece.shape[0]
    width_now = code_piece.shape[1]
    blocked = (
        code_piece.astype(jnp.float32).reshape(block_count, -1, width_now)
        * scale_piece.astype(jnp.float32)[:, None, :]
    )
    return blocked.reshape(code_piece.shape).astype(jnp.bfloat16)


def body(tokens, cotangent, codes, scales, adapter_down, adapter_up):
    inv_root = 1.0 / math.sqrt(MODEL_WIDTH)
    entire_width = adapter_up.shape[1]
    down_lowered = adapter_down.astype(jnp.bfloat16)
    rank_portion = jnp.dot(tokens, down_lowered, preferred_element_type=jnp.float32) * inv_root
    adapter_branch_output = adapter_scale * jnp.dot(
        rank_portion, adapter_up, precision=lax.Precision.HIGHEST
    )
    wide_cotangent = cotangent.astype(jnp.float32)
    rank_backward = adapter_scale * jnp.dot(
        wide_cotangent, adapter_up.T, precision=lax.Precision.HIGHEST
    )
    back_low = rank_backward.astype(jnp.bfloat16)
    beside = (
        jnp.einsum("tr,kr->tk", back_low, down_lowered, preferred_element_type=jnp.float32)
        * inv_root
    )
    whole_codes, whole_scales = (
        lax.all_gather(codes, "fsdp", axis=1, tiled=True),
        lax.all_gather(scales, "fsdp", axis=1, tiled=True),
    )
    weight = dequant(whole_codes, whole_scales)
    main_part = jnp.dot(tokens, weight, preferred_element_type=jnp.float32)
    grad_wide = beside + jnp.einsum(
        "tn,kn->tk", cotangent, weight, preferred_element_type=jnp.float32
    )
    values = lax.psum_scatter(
        main_part + adapter_branch_output, "tp", scatter_dimension=1, tiled=True
    ).astype(jnp.bfloat16)
    grad_tokens = grad_wide.astype(jnp.bfloat16)
    down_gradient = (
        jnp.einsum("tk,tr->kr", tokens, back_low, preferred_element_type=jnp.float32) * inv_root
    )
    up_gradient_portion = adapter_scale * jnp.dot(
        rank_portion.T, wide_cotangent, precision=lax.Precision.HIGHEST
    )
    down_gradient_sum, summed_b = lax.psum((down_gradient, up_gradient_portion), ("rep", "fsdp"))
    refreshed_down = adapter_down - down_learning_rate * norm_divided(down_gradient_sum, 1)
    whole_a = lax.all_gather(refreshed_down.astype(jnp.bfloat16), "tp", axis=0, tiled=True)
    column_total = entire_width // lax.axis_size("tp")
    leading_column = lax.axis_index("tp") * column_total
    b_parts = lax.all_gather(summed_b[None].astype(jnp.bfloat16), "tp", axis=0, tiled=True).astype(
        jnp.float32
    )
    up_gradient = lax.dynamic_slice_in_dim(
        jnp.sum(b_parts, axis=0), leading_column, column_total, 1
    )
    primary_columns = lax.dynamic_slice_in_dim(adapter_up, leading_column, column_total, 1)
    refreshed_up = primary_columns - up_learning_rate * norm_divided(up_gradient, 0)
    return (values, grad_tokens, refreshed_down, whole_a, refreshed_up)


def solution(mesh):
    in_specs = (
        P(("rep", "fsdp"), "tp"),
        P(("rep", "fsdp"), None),
        P("tp", "fsdp"),
        P("tp", "fsdp"),
        P("tp", None),
        P(),
    )
    out_specs = (
        P(("rep", "fsdp"), "tp"),
        P(("rep", "fsdp"), "tp"),
        P("tp", None),
        P(),
        P(None, "tp"),
    )
    return jax.shard_map(body, mesh=mesh, in_specs=in_specs, out_specs=out_specs, check_vma=False)
```

profile of v0, /device:TPU:1, one launch (start us, length us, event | category | flops | bytes accessed | tf_op | source)
XLA Modules:
  0.0 808.5 jit_solution(14206771136499768052)
XLA Ops:
  8.1 1.8 fusion.5
  9.9 1.1 fusion.3
  11.1 0.5 all-gather.5.cloned.1.call-update
  11.7 244.4 %all-reduce.3.cloned.1.call-done = f32[2048,64]{0,1:T(8,128)} async-done(((f32[2048,64]{0,1:T(8,128)}), f32[2048,64]{0,1:T(8,128)}) %all-reduce.3.cloned.1.call-update) | async-done | bytes 524304 | tf_op jit(solution)/shard_map/psum | solution.py:67
  256.1 1.1 multiply_reduce_fusion
  257.2 2.2 fusion.10
  259.4 25.3 %all-gather.1 = bf16[16,64,16]{1,2,0:T(8,128)(2,1)S(1)} all-gather(bf16[1,64,16]{1,2,0:T(8,128)(2,1)S(1)} %bitcast.39), channel_id=1, replica_groups=mesh['rep'=8,'fsdp'=16,'tp'=4] {'fsdp'}, dimensions={0}, use_global_device_ids=true | all-gather | bytes 34816 | tf_op jit(solution)/shard_map/all_gather | solution.py:50
  284.8 0.1 reshape.35
  284.9 0.2 copy.20
  285.1 0.4 convolution_multiply_fusion.5
  285.6 2.3 mul.81
  287.9 2.7 convolution_bitcast_fusion.1
  290.7 0.4 copy-done.1
  291.1 2.1 fusion.4
  293.2 0.4 convolution_multiply_fusion.3
  293.6 484.2 %all-reduce.4 = bf16[64,1024]{1,0:T(8,128)(2,1)S(1)} all-reduce(f32[64,1024]{1,0:T(8,128)S(1)} %convolution_multiply_fusion.3), channel_id=1, replica_groups=mesh['rep'=8,'fsdp'=16,'tp'=4] {'rep','fsdp'}, use_global_device_ids=true, to_apply=%region_3.0 | all-reduce | flops 65536 | bytes 393216 | tf_op jit(solution)/shard_map/psum | solution.py:67
  777.8 10.5 %all-gather = bf16[256,1024]{1,0:T(8,128)(2,1)S(1)} all-gather(bf16[64,1024]{1,0:T(8,128)(2,1)S(1)} %all-reduce.4), channel_id=2, replica_groups=mesh['rep'=8,'fsdp'=16,'tp'=4] {'tp'}, dimensions={0}, use_global_device_ids=true | all-gather | bytes 655360 | tf_op jit(solution)/shard_map/all_gather | solution.py:72
  788.3 0.1 convert_reduce_fusion
  788.4 0.7 multiply_subtract_fusion.1
  789.1 7.7 convolution_bitcast_fusion
  796.8 1.4 fusion.2
  798.2 1.0 convert_element_type.38
  799.2 0.8 copy.23
  799.9 1.0 copy.34
  (29 shorter events, 0.4 us)
Async XLA Ops:
  8.0 1.9 copy-start
  8.0 277.1 %copy-start.3 = (f32[2048,64]{0,1:T(8,128)S(1)}, f32[2048,64]{0,1:T(8,128)}, u32[]{:S(2)}) copy-start(f32[2048,64]{0,1:T(8,128)} %param.10) | copy-start | bytes 1572868
  8.0 251.4 %copy-start.7 = (bf16[16,64]{1,0:T(8,128)(2,1)S(1)}, bf16[16,64]{1,0:T(8,128)(2,1)}, u32[]{:S(2)}) copy-start(bf16[16,64]{1,0:T(8,128)(2,1)} %param.9) | copy-start | bytes 6148
  8.0 248.0 %all-reduce.3.cloned.1.call-start = ((), (), s32[]{:S(2)}) async-start(), calls=%async_computation.3 | async-start | bytes 1048576 | tf_op jit(solution)/shard_map/psum | solution.py:67
  11.0 274.5 %all-gather.5.cloned.1.call-start = ((), (), s32[]{:S(2)}) async-start(), calls=%async_computation.1 | async-start | bytes 4456448 | tf_op jit(solution)/shard_map/all_gather | solution.py:49
  11.6 777.5 %all-gather.7.cloned.1.call-start = ((), (), s32[]{:S(2)}) async-start(), calls=%async_computation.4 | async-start | bytes 1310720 | tf_op jit(solution)/shard_map/all_gather | solution.py:69
  259.3 538.8 %reduce-scatter.2.cloned.1.call-start = ((), (), s32[]{:S(2)}) async-start(), calls=%async_computation.2 | async-start | bytes 1310720 | tf_op jit(solution)/shard_map/reduce_scatter | solution.py:57
  285.6 2.3 copy-start.2
  287.9 3.2 copy-start.1
  287.9 3.2 copy-start.5
  287.9 5.3 copy-start.4
  796.7 3.2 copy-start.6
Sparse Core Ops, SparseCore 0:
  12.7 243.3 all-reduce.2
Sparse Core Ops, SparseCore 1:
  13.6 106.7 all-gather.4
  259.4 25.3 all-gather.6
  293.3 31.5 reduce-scatter.1
where the time goes:
time: 825 us; the launch traced here: 808 us
  blocking collectives  520 us (63%)
  waiting for transfers between devices  245 us (30%)
  matrix products  17.6 us (2%)
  between operations  15.8 us (2%)
    psum x1, blocking collectives, body(): lax.psum((down_gradient, up_gradient_portion), ('rep', 'fsdp'))  484 us
    psum x1, waiting for transfers between devices, body(): lax.psum((down_gradient, up_gradient_portion), ('rep', 'fsdp'))  244 us
    all_gather x1, blocking collectives, body(): lax.all_gather(scales, 'fsdp', axis=1, tiled=True)  25.3 us
  transfers between devices with their start and end apart: 4, of which 1 were waited for; matrix products, arithmetic and copies ran while one was open for 3% of the time, Pallas kernels for 0%

commit v1 on v0

v1 whole, which is shorter than its diff:
```python
import math

import jax
import jax.numpy as jnp
from jax import lax
from jax.experimental import pallas as pl
from jax.experimental.pallas import tpu as pltpu
from jax.sharding import Mesh
from jax.sharding import PartitionSpec as P

MODEL_WIDTH = 8192
QB = 128
INV_ROOT = 1.0 / math.sqrt(MODEL_WIDTH)

adapter_scale = 0.25
down_learning_rate = 1.0
up_learning_rate = 0.1
eps_norm = 1e-06

f32 = jnp.float32
bf16 = jnp.bfloat16
PLANE = ("zh", "y", "zl")
LIMIT = 48 * 1024 * 1024

NN = (((1,), (0,)), ((), ()))
NT = (((1,), (1,)), ((), ()))
TN = (((0,), (0,)), ((), ()))


def dot(a, b, dims):
    return lax.dot_general(a, b, dims, preferred_element_type=f32)


def thirds(a):
    high = a.astype(bf16)
    rest = a - high.astype(f32)
    middle = rest.astype(bf16)
    return high, middle, (rest - middle.astype(f32)).astype(bf16)


def call(kernel, outs, scalars, arrays, flops=0):
    return pl.pallas_call(
        kernel,
        out_shape=outs,
        in_specs=[pl.BlockSpec(memory_space=pltpu.SMEM)] * len(scalars)
        + [pl.BlockSpec(memory_space=pltpu.VMEM)] * len(arrays),
        out_specs=jax.tree.map(lambda _: pl.BlockSpec(memory_space=pltpu.VMEM), outs),
        compiler_params=pltpu.CompilerParams(vmem_limit_bytes=LIMIT),
        cost_estimate=pl.CostEstimate(flops=flops, bytes_accessed=1 << 20, transcendentals=0),
    )(*scalars, *arrays)


def shape(*dims, dtype=f32):
    return jax.ShapeDtypeStruct(dims, dtype)


def halves(core, width):
    first = pl.multiple_of(core * width, width)
    return pl.ds(first, width), pl.ds(pl.multiple_of(width - first, width), width)


def store_tiles(ref, wide):
    rows, columns = wide.shape[0] // 8, wide.shape[1] // 128
    for i in range(rows):
        for j in range(columns):
            ref[i * columns + j] = wide[8 * i : 8 * i + 8, 128 * j : 128 * j + 128]


def load_tiles(ref, first, columns):
    rows = [
        jnp.concatenate([ref[i * columns + j, first : first + 8] for j in range(columns)], axis=1)
        for i in range(8)
    ]
    return jnp.concatenate(rows, axis=0)


def down_gradient_kernel(core, tokens, cotangent, up, low_ref, keep_ref, send_ref):
    high, middle, low = thirds(up[...])
    wide = cotangent[...]
    back = dot(wide, low, NT) + dot(wide, middle, NT) + dot(wide, high, NT)
    back_low = (adapter_scale * back).astype(bf16)
    low_ref[...] = back_low
    own, other = halves(core[0], tokens.shape[1] // 2)
    store_tiles(send_ref, dot(back_low, tokens[:, other], TN) * INV_ROOT)
    store_tiles(keep_ref, dot(back_low, tokens[:, own], TN) * INV_ROOT)


def up_gradient_kernel(tokens, down, cotangent, rank_ref, tiles_ref):
    rank = dot(tokens[...], down[...].astype(bf16), NT) * INV_ROOT
    rank_ref[...] = rank
    high, middle, low = thirds(rank)
    wide = cotangent[...]
    store_tiles(
        tiles_ref, adapter_scale * (dot(low, wide, TN) + dot(middle, wide, TN) + dot(high, wide, TN))
    )


def total_kernel(parts, out):
    total = parts[0]
    for i in range(1, parts.shape[0]):
        total = total + parts[i]
    for i in range(parts.shape[0]):
        out[i] = total


def normed(grad):
    mean = jnp.mean(grad * grad, axis=0, keepdims=True)
    return grad * lax.rsqrt(mean + eps_norm)


def scorer_kernel(core, gathered, down, out, raw_ref):
    own, _ = halves(core[0], down.shape[1] // 2)
    grad = load_tiles(gathered, 0, 8)
    raw_ref[...] = grad
    fresh = (down[:, own] - down_learning_rate * normed(grad)).astype(bf16)
    up_grad = load_tiles(gathered, 8, 8).astype(bf16)
    for p in range(4):
        out[p, :, :1024] = fresh
        out[p, :, 1024:] = up_grad[:, 256 * p : 256 * p + 256]


def down_kernel(core, raw, raw_other, down, out):
    own, other = halves(core[0], down.shape[1] // 2)
    out[:, own] = down[:, own] - down_learning_rate * normed(raw[...])
    out[:, other] = down[:, other] - down_learning_rate * normed(raw_other[...])


def finish_kernel(core, place, rows, rows_other, part, part_other, up, scorer_ref, up_ref):
    first = core[0] == 0
    for p in range(4):
        mine, theirs = rows[p], rows_other[p]
        scorer_ref[2048 * p : 2048 * p + 1024, :] = jnp.where(first, mine, theirs).T
        scorer_ref[2048 * p + 1024 : 2048 * p + 2048, :] = jnp.where(first, theirs, mine).T
    columns = pl.ds(pl.multiple_of(place[0] * 256, 256), 256)
    up_ref[...] = up[:, columns] - up_learning_rate * normed(part[...] + part_other[...])


def near_values_kernel(core, tokens, weight, rank, up, out):
    own, _ = halves(core[0], tokens.shape[1] // 2)
    branch = lax.dot_general(
        rank[...], up[...], NN, precision=lax.Precision.HIGHEST, preferred_element_type=f32
    )
    out[...] = dot(tokens[:, own], weight[...], NT) + adapter_scale * branch


def far_values_kernel(core, tokens, weight, near, out):
    _, other = halves(core[0], tokens.shape[1] // 2)
    whole = near[...] + dot(tokens[:, other], weight[...], NT)
    for p in range(4):
        out[p] = whole[:, 256 * p : 256 * p + 256]


def token_gradient_kernel(core, cotangent, near, far, back_low, down, out):
    own, other = halves(core[0], down.shape[1] // 2)
    for place, weight in ((own, near), (other, far)):
        beside = dot(back_low[...], down[:, place].astype(bf16), NN) * INV_ROOT
        out[:, place] = (dot(cotangent[...], weight[...], NN) + beside).astype(bf16)


def body(tokens, cotangent, codes, scales, adapter_down, adapter_up):
    core_at = lax.axis_index("c")
    core = core_at.astype(jnp.int32).reshape(1)
    place = lax.axis_index("x").astype(jnp.int32).reshape(1)
    down = adapter_down.T
    swap = [(0, 1), (1, 0)]
    half = codes.shape[0] // 2

    with jax.named_scope("dequant"):
        code_half = lax.dynamic_slice_in_dim(codes.T, core_at * half, half, 1)
        scale_half = lax.dynamic_slice_in_dim(scales.T, core_at * (half // QB), half // QB, 1)
        blocked = code_half.astype(f32).reshape(-1, half // QB, QB) * scale_half.astype(f32)[:, :, None]
        mine = blocked.reshape(code_half.shape).astype(bf16)
        theirs = lax.ppermute(mine, "zl", swap)
        low_first = lax.axis_index("zl") == 0
        pair = jnp.concatenate(
            [jnp.where(low_first, mine, theirs), jnp.where(low_first, theirs, mine)], axis=0
        )
    with jax.named_scope("weight_gather"):
        near = lax.all_gather(pair, "y", axis=0, tiled=True)
        far = lax.ppermute(near, "c", swap)

    with jax.named_scope("gradients"):
        back_low, keep, send = call(
            down_gradient_kernel,
            (shape(256, 64, dtype=bf16), shape(64, 8, 128), shape(64, 8, 128)),
            (core,),
            (tokens, cotangent, adapter_up),
        )
        arrived = lax.ppermute(send, "c", swap)
        rank, up_tiles = call(
            up_gradient_kernel, (shape(256, 64), shape(64, 8, 128)), (), (tokens, down, cotangent)
        )
    with jax.named_scope("plane_sum"):
        parts = jnp.concatenate([keep + arrived, up_tiles], axis=1)
        parts = lax.all_to_all(parts, PLANE, 0, 0, tiled=True)
        total = call(total_kernel, shape(64, 16, 128), (), (parts,))
        gathered = lax.all_to_all(total, PLANE, 0, 0, tiled=True)
    with jax.named_scope("refresh"):
        rows, raw = call(
            scorer_kernel, (shape(4, 64, 1280, dtype=bf16), shape(64, 1024)), (core,), (gathered, down)
        )
        raw_other = lax.ppermute(raw, "c", swap)
        rows = lax.all_to_all(rows, "x", 0, 0, tiled=True)
        part = jnp.sum(rows[:, :, 1024:].astype(f32), axis=0)
        rows = rows[:, :, :1024]
        rows_other = lax.ppermute(rows, "c", swap)
        part_other = lax.ppermute(part, "c", swap)
        refreshed_down = call(
            down_kernel, shape(64, 2048), (core,), (raw, raw_other, down)
        ).T
        scorer_a, refreshed_up = call(
            finish_kernel,
            (shape(8192, 64, dtype=bf16), shape(64, 256)),
            (core, place),
            (rows, rows_other, part, part_other, adapter_up),
        )
    with jax.named_scope("values"):
        near_part = call(
            near_values_kernel, shape(256, 1024), (core,), (tokens, near, rank, adapter_up)
        )
        whole = call(far_values_kernel, shape(4, 256, 256), (core,), (tokens, far, near_part))
        at = lax.axis_index("x")
        values = lax.dynamic_index_in_dim(whole, at, 0, keepdims=False)
        for k in range(1, 4):
            out = lax.dynamic_index_in_dim(whole, (at + k) % 4, 0, keepdims=False)
            values = values + lax.ppermute(out, "x", [(i, (i + k) % 4) for i in range(4)])
        values = values.astype(bf16)
    with jax.named_scope("grad_tokens"):
        grad_tokens = call(
            token_gradient_kernel,
            shape(256, 2048, dtype=bf16),
            (core,),
            (cotangent, near, far, back_low, down),
        )
    return (values, grad_tokens, refreshed_down, scorer_a, refreshed_up)


def solution(mesh):
    fine = Mesh(mesh.devices.reshape(4, 2, 8, 2, 4), ("zh", "c", "y", "zl", "x"))
    tokens_at = ("zh", "c", "y", "zl")
    in_specs = (
        P(tokens_at, "x"),
        P(tokens_at, None),
        P("x", ("y", "zl")),
        P("x", ("y", "zl")),
        P("x", None),
        P(),
    )
    out_specs = (
        P(tokens_at, "x"),
        P(tokens_at, "x"),
        P("x", None),
        P(),
        P(None, "x"),
    )
    return jax.shard_map(body, mesh=fine, in_specs=in_specs, out_specs=out_specs, check_vma=False)
```

time: 825 us -> 169 us (0.20); the launches traced: 808 us -> 168 us
  blocking collectives: 520 us -> 39.6 us
  waiting for transfers between devices: 245 us -> 35.1 us
  starting transfers between devices: 0.17 us -> 47.9 us
  matrix products: 17.6 us -> 0 us
  Pallas kernels: 0 us -> 13.7 us
    psum x1 -> x0, blocking collectives: 484 us -> none  [body(): lax.psum((down_gradient, up_gradient_portion), ('rep', 'fsdp'))]
    psum x1 -> x0, waiting for transfers between devices: 244 us -> none  [body(): lax.psum((down_gradient, up_gradient_portion), ('rep', 'fsdp'))]
    all_to_all x0 -> x2, blocking collectives: none -> 39.6 us  [the longest x1 27.7 us: body(): gathered = lax.all_to_all(total, PLANE, 0, 0, tiled=True)]
    ppermute x0 -> x9, starting transfers between devices: none -> 36.7 us  [the longest x1 8.47 us: body(): arrived = lax.ppermute(send, 'c', swap)]
    all_gather x2 -> x0, blocking collectives: 35.8 us -> none  [the longest x1 25.3 us: body(): lax.all_gather(scales, 'fsdp', axis=1, tiled=True)]
    all_gather x2 -> x1, waiting for transfers between devices: 0.03 us -> 32.7 us  [body(): near = lax.all_gather(pair, 'y', axis=0, tiled=True)]
    dot_general x8 -> x0, matrix products: 17.6 us -> none  [the longest x1 7.67 us: body(): jnp.einsum('tn,kn->tk', cotangent, weight, preferred_element_type=jnp.flo...]
    pallas_call x0 -> x9, Pallas kernels: none -> 13.7 us  [call(): pl.pallas_call(kernel, out_shape=outs, in_specs=[pl.BlockSpec(memory_spac...]
  transfers between devices with their start and end apart: 4 -> 11, of which waited for: 1 -> 2; matrix products, arithmetic and copies ran while one was open for 3% -> 4% of each run, Pallas kernels for 0% -> 8%
where the time goes in v1:
time: 169 us; the launch traced here: 168 us
  starting transfers between devices  47.9 us (28%)
  blocking collectives  39.6 us (23%)
  waiting for transfers between devices  35.1 us (21%)
  between operations  14.4 us (9%)
  Pallas kernels  13.7 us (8%)
  local copies, waits for them, and re-layouts  10.9 us (6%)
  other arithmetic  6.24 us (4%)
    all_gather x1, waiting for transfers between devices, body(): near = lax.all_gather(pair, 'y', axis=0, tiled=True)  32.7 us
    all_to_all x1, blocking collectives, body(): gathered = lax.all_to_all(total, PLANE, 0, 0, tiled=True)  27.7 us
    pallas_call x9, Pallas kernels, call(): pl.pallas_call(kernel, out_shape=outs, in_specs=[pl.BlockSpec(memory_spac...  13.7 us
    all_to_all x1, blocking collectives, body(): rows = lax.all_to_all(rows, 'x', 0, 0, tiled=True)  11.8 us
    all_to_all x1, starting transfers between devices, body(): parts = lax.all_to_all(parts, PLANE, 0, 0, tiled=True)  11.2 us
    unnamed x37, local copies, waits for them, and re-layouts  8.89 us
    ppermute x1, starting transfers between devices, body(): arrived = lax.ppermute(send, 'c', swap)  8.47 us
    ppermute x3, starting transfers between devices, body(): lax.ppermute(out, 'x', [(i, (i + k) % 4) for i in range(4)])  7.8 us
  transfers between devices with their start and end apart: 11, of which 2 were waited for; matrix products, arithmetic and copies ran while one was open for 4% of the time, Pallas kernels for 8%

profile of v1, /device:TPU:1, one launch (start us, length us, event | category | flops | bytes accessed | tf_op | source)
XLA Modules:
  0.0 167.9 jit_solution(1526546056864279133)
XLA Ops:
  9.3 4.8 %collective-permute-start = (bf16[64,1024]{1,0:T(8,128)(2,1)S(1)}, bf16[64,1024]{1,0:T(8,128)(2,1)S(1)}, u32[]{:S(2)}, u32[]{:S(2)}) collective-permute-start(bf16[64,1024]{1,0:T(8,128)(2,1)S(1)} %fusion), channel_id=1, source_target_pairs={{0,4},{4,0},{1,5},{5,1},{2,6},{6,2},{3,7},{7,3},{8,12},{12,8},{9,1... | collective-permute-start | bytes 393224 | tf_op jit(solution)/shard_map/dequant/ppermute | solution.py:173
  14.1 2.3 %collective-permute-done = bf16[64,1024]{1,0:T(8,128)(2,1)S(1)} collective-permute-done((bf16[64,1024]{1,0:T(8,128)(2,1)S(1)}, bf16[64,1024]{1,0:T(8,128)(2,1)S(1)}, u32[]{:S(2)}, u32[]{:S(2)}) %collective-permute-start) | collective-permute-done | bytes 131104 | tf_op jit(solution)/shard_map/dequant/ppermute | solution.py:173
  17.3 1.1 gradients.3
  18.4 8.5 %collective-permute-start.5 = (f32[64,8,128]{2,1,0:T(8,128)S(1)}, f32[64,8,128]{2,1,0:T(8,128)S(1)}, u32[]{:S(2)}, u32[]{:S(2)}) collective-permute-start(f32[64,8,128]{2,1,0:T(8,128)S(1)} %get-tuple-element.17), channel_id=1, source_target_pairs={{0,64},{64,0},{1,65},{65,1},{2,66},{66,2},{3,67},{67,3},{4,68},{68... | collective-permute-start | bytes 786440 | tf_op jit(solution)/shard_map/gradients/ppermute | solution.py:189
  26.9 1.2 gradients.2
  29.0 11.2 %all-to-all-start = ((f32[64,16,128]{2,1,0:T(8,128)}), f32[64,16,128]{2,1,0:T(8,128)S(1)}, u32[]{:S(2)}, u32[]{:S(2)}) async-start(f32[64,16,128]{2,1,0:T(8,128)} %pad_maximum_fusion), calls=%async_computation | async-start | bytes 1048576 | tf_op jit(solution)/shard_map/plane_sum/all_to_all | solution.py:195
  40.2 32.7 %all-gather.2.cloned.1.call-done.weight.near = bf16[1024,1024]{1,0:T(8,128)(2,1)} async-done(((bf16[128,1024]{1,0:T(8,128)(2,1)}), bf16[1024,1024]{1,0:T(8,128)(2,1)}) %all-gather.2.cloned.1.call-update) | async-done | bytes 2097168 | tf_op jit(solution)/shard_map/weight_gather/all_gather | solution.py:179
  72.9 5.4 %collective-permute-start.1 = (bf16[1024,1024]{1,0:T(8,128)(2,1)}, bf16[1024,1024]{1,0:T(8,128)(2,1)}, u32[]{:S(2)}, u32[]{:S(2)}) collective-permute-start(bf16[1024,1024]{1,0:T(8,128)(2,1)} %all-gather.2.cloned.1.call-done.weight.near), channel_id=1, source_target_pairs={{0,64},{64,0},{1,65},{65,1},{2,66},{66,2},{3,67},{67,3},{4,68},{68... | collective-permute-start | bytes 6291464 | tf_op jit(solution)/shard_map/weight_gather/ppermute | solution.py:180
  78.5 27.7 %all_to_all.15.gathered = f32[64,16,128]{2,1,0:T(8,128)S(1)} all-to-all(f32[64,16,128]{2,1,0:T(8,128)S(1)} %plane_sum.1), channel_id=1, replica_groups=mesh['zh'=4,'c'=2,'y'=8,'zl'=2,'x'=4] {'zh','y','zl'}, dimensions={0} | all-to-all | bytes 1048576 | tf_op jit(solution)/shard_map/plane_sum/all_to_all | solution.py:197
  106.2 1.0 copy-done.3
  107.4 11.8 %all_to_all.16 = bf16[4,64,1280]{2,1,0:T(8,128)(2,1)S(1)} all-to-all(bf16[4,64,1280]{2,1,0:T(8,128)(2,1)S(1)} %get-tuple-element.20), channel_id=1, replica_groups=mesh['zh'=4,'c'=2,'y'=8,'zl'=2,'x'=4] {'x'}, dimensions={0} | all-to-all | bytes 1310720 | tf_op jit(solution)/shard_map/refresh/all_to_all | solution.py:203
  120.2 5.2 %collective-permute-start.7 = (bf16[4,64,1024]{2,1,0:T(8,128)(2,1)}, bf16[4,64,1024]{2,1,0:T(8,128)(2,1)}, u32[]{:S(2)}, u32[]{:S(2)}) collective-permute-start(bf16[4,64,1024]{2,1,0:T(8,128)(2,1)} %slice.8.rows), channel_id=1, source_target_pairs={{0,64},{64,0},{1,65},{65,1},{2,66},{66,2},{3,67},{67,3},{4,68},{68... | collective-permute-start | bytes 1572872 | tf_op jit(solution)/shard_map/refresh/ppermute | solution.py:206
  125.5 1.9 %collective-permute-start.6 = (f32[64,1024]{1,0:T(8,128)}, f32[64,1024]{1,0:T(8,128)S(1)}, u32[]{:S(2)}, u32[]{:S(2)}) collective-permute-start(f32[64,1024]{1,0:T(8,128)} %copy-done.11), channel_id=1, source_target_pairs={{0,64},{64,0},{1,65},{65,1},{2,66},{66,2},{3,67},{67,3},{4,68},{68... | collective-permute-start | bytes 786440 | tf_op jit(solution)/shard_map/refresh/ppermute | solution.py:202
  127.5 1.5 values.2.near
  129.0 2.3 %values.3 = f32[4,256,256]{2,1,0:T(8,128)S(1)} custom-call(s32[1]{0:T(128)} %bitcast.core, bf16[256,2048]{1,0:T(8,128)(2,1)S(1)} %copy-done, bf16[1024,1024]{1,0:T(8,128)(2,1)} %collective-permute-done.1.weight.far, f32[256,1024]{1,0:T(8,128)S(1)} %values.2.near), custom_call_target="tpu_custom_call" | custom-call | bytes 1048576 | tf_op jit(solution)/shard_map/values/pallas_call | solution.py:42
  133.2 2.8 %collective-permute-start.4 = (f32[256,256]{1,0:T(8,128)}, f32[256,256]{1,0:T(8,128)}, u32[]{:S(2)}, u32[]{:S(2)}) collective-permute-start(f32[256,256]{1,0:T(8,128)} %get-tuple-element.29), channel_id=1, source_target_pairs={{0,3},{1,0},{2,1},{3,2},{4,7},{5,4},{6,5},{7,6},{8,11},{9,8},{10,9... | collective-permute-start | bytes 786440 | tf_op jit(solution)/shard_map/values/ppermute | solution.py:226
  136.0 3.1 %collective-permute-start.3 = (f32[256,256]{1,0:T(8,128)}, f32[256,256]{1,0:T(8,128)}, u32[]{:S(2)}, u32[]{:S(2)}) collective-permute-start(f32[256,256]{1,0:T(8,128)} %get-tuple-element.30), channel_id=1, source_target_pairs={{0,2},{1,3},{2,0},{3,1},{4,6},{5,7},{6,4},{7,5},{8,10},{9,11},{10,... | collective-permute-start | bytes 786440 | tf_op jit(solution)/shard_map/values/ppermute | solution.py:226
  139.1 1.9 %collective-permute-start.2 = (f32[256,256]{1,0:T(8,128)}, f32[256,256]{1,0:T(8,128)}, u32[]{:S(2)}, u32[]{:S(2)}) collective-permute-start(f32[256,256]{1,0:T(8,128)} %get-tuple-element.28), channel_id=1, source_target_pairs={{0,1},{1,2},{2,3},{3,0},{4,5},{5,6},{6,7},{7,4},{8,9},{9,10},{10,1... | collective-permute-start | bytes 786440 | tf_op jit(solution)/shard_map/values/ppermute | solution.py:226
  142.7 3.0 %collective-permute-start.8 = (f32[64,256]{1,0:T(8,128)S(1)}, f32[64,256]{1,0:T(8,128)S(1)}, u32[]{:S(2)}, u32[]{:S(2)}) collective-permute-start(f32[64,256]{1,0:T(8,128)S(1)} %convert_reduce_fusion.part), channel_id=1, source_target_pairs={{0,64},{64,0},{1,65},{65,1},{2,66},{66,2},{3,67},{67,3},{4,68},{68... | collective-permute-start | bytes 196616 | tf_op jit(solution)/shard_map/refresh/ppermute | solution.py:207
  148.5 2.4 %refresh.5 = (bf16[8192,64]{1,0:T(8,128)(2,1)S(1)}, f32[64,256]{1,0:T(8,128)}) custom-call(s32[1]{0:T(128)} %bitcast.core, s32[1]{0:T(128)} %bitcast.9.place, bf16[4,64,1024]{2,1,0:T(8,128)(2,1)} %slice.8.rows, bf16[4,64,1024]{2,1,0:T(8,128)(2,1)} %collective-permute-done.7.rows_other, f32[64,256]{1,0:T(8,128)S(1)} %convert_reduce_fusion.part, ...), custom_call_target="tpu_custom_call" | custom-call | bytes 1048576 | tf_op jit(solution)/shard_map/refresh/pallas_call | solution.py:42
  150.9 1.4 copy-done.10
  152.3 2.8 %copy.12 = bf16[8192,64]{0,1:T(8,128)(2,1)} copy(bf16[8192,64]{1,0:T(8,128)(2,1)} %copy-done.10) | data formatting | bytes 2097152
  155.1 4.1 %grad_tokens.1 = bf16[256,2048]{1,0:T(8,128)(2,1)} custom-call(s32[1]{0:T(128)} %bitcast.core, bf16[256,1024]{1,0:T(8,128)(2,1)S(1)} %copy-done.7, bf16[1024,1024]{1,0:T(8,128)(2,1)S(1)} %copy-done.1, bf16[1024,1024]{1,0:T(8,128)(2,1)} %collective-permute-done.1.weight.far, bf16[256,64]{1,0:T(8,128)(2,1)S(1)} %copy-done.16, f32[64,2048]{1,0:T(8,128)S(1)} %bitcast.30), custom_call_target="tpu_custom_call" | custom-call | bytes 1048576 | tf_op jit(solution)/shard_map/grad_tokens/pallas_call | solution.py:42
  159.2 1.9 %fusion.3 = bf16[256,256]{1,0:T(8,128)(2,1)} fusion(f32[256,256]{1,0:T(8,128)} %collective-permute-done.4, f32[256,256]{1,0:T(8,128)} %collective-permute-done.3, f32[256,256]{1,0:T(8,128)} %collective-permute-done.2, f32[4,256,256]{2,1,0:T(8,128)} %copy-done.8, s32[]{:T(128)S(6)} %select_n.51), kind=kLoop, calls=%fused_computation.7 | loop fusion | flops 262144 | bytes 1179652 | tf_op jit(solution)/shard_map/values/convert_element_type | solution.py:227
  (59 shorter events, 11.2 us)
Async XLA Ops:
  7.2 10.1 %copy-start = (bf16[256,2048]{1,0:T(8,128)(2,1)S(1)}, bf16[256,2048]{1,0:T(8,128)(2,1)}, u32[]{:S(2)}) copy-start(bf16[256,2048]{1,0:T(8,128)(2,1)} %tokens.7) | copy-start | bytes 3145732
  7.2 10.1 %copy-start.6 = (bf16[256,1024]{1,0:T(8,128)(2,1)S(1)}, bf16[256,1024]{1,0:T(8,128)(2,1)}, u32[]{:S(2)}) copy-start(bf16[256,1024]{1,0:T(8,128)(2,1)} %cotangent.5) | copy-start | bytes 1572868
  7.2 10.1 %copy-start.9 = (f32[64,1024]{1,0:T(8,128)S(1)}, f32[64,1024]{1,0:T(8,128)}, u32[]{:S(2)}) copy-start(f32[64,1024]{1,0:T(8,128)} %up.5) | copy-start | bytes 786436
  7.2 19.7 %copy-start.2 = (f32[2048,64]{0,1:T(8,128)S(1)}, f32[2048,64]{0,1:T(8,128)}, u32[]{:S(2)}) copy-start(f32[2048,64]{0,1:T(8,128)} %param.10) | copy-start | bytes 1572868
  7.2 65.7 %all-gather.2.cloned.1.call-start = ((), (), s32[]{:S(2)}) async-start(), calls=%async_computation.3 | async-start | bytes 2359296 | tf_op jit(solution)/shard_map/weight_gather/all_gather | solution.py:179
  9.3 7.2 %collective-permute-start = (bf16[64,1024]{1,0:T(8,128)(2,1)S(1)}, bf16[64,1024]{1,0:T(8,128)(2,1)S(1)}, u32[]{:S(2)}, u32[]{:S(2)}) collective-permute-start(bf16[64,1024]{1,0:T(8,128)(2,1)S(1)} %fusion), channel_id=1, source_target_pairs={{0,4},{4,0},{1,5},{5,1},{2,6},{6,2},{3,7},{7,3},{8,12},{12,8},{9,1... | collective-permute-start | bytes 393224 | tf_op jit(solution)/shard_map/dequant/ppermute | solution.py:173
  18.4 10.6 %copy-start.15 = (bf16[256,64]{1,0:T(8,128)(2,1)}, bf16[256,64]{1,0:T(8,128)(2,1)S(1)}, u32[]{:S(2)}) copy-start(bf16[256,64]{1,0:T(8,128)(2,1)S(1)} %get-tuple-element.15.back_low) | copy-start | bytes 98308
  18.4 9.7 %collective-permute-start.5 = (f32[64,8,128]{2,1,0:T(8,128)S(1)}, f32[64,8,128]{2,1,0:T(8,128)S(1)}, u32[]{:S(2)}, u32[]{:S(2)}) collective-permute-start(f32[64,8,128]{2,1,0:T(8,128)S(1)} %get-tuple-element.17), channel_id=1, source_target_pairs={{0,64},{64,0},{1,65},{65,1},{2,66},{66,2},{3,67},{67,3},{4,68},{68... | collective-permute-start | bytes 786440 | tf_op jit(solution)/shard_map/gradients/ppermute | solution.py:189
  29.0 49.4 %all-to-all-start = ((f32[64,16,128]{2,1,0:T(8,128)}), f32[64,16,128]{2,1,0:T(8,128)S(1)}, u32[]{:S(2)}, u32[]{:S(2)}) async-start(f32[64,16,128]{2,1,0:T(8,128)} %pad_maximum_fusion), calls=%async_computation | async-start | bytes 1048576 | tf_op jit(solution)/shard_map/plane_sum/all_to_all | solution.py:195
  72.9 56.1 %collective-permute-start.1 = (bf16[1024,1024]{1,0:T(8,128)(2,1)}, bf16[1024,1024]{1,0:T(8,128)(2,1)}, u32[]{:S(2)}, u32[]{:S(2)}) collective-permute-start(bf16[1024,1024]{1,0:T(8,128)(2,1)} %all-gather.2.cloned.1.call-done.weight.near), channel_id=1, source_target_pairs={{0,64},{64,0},{1,65},{65,1},{2,66},{66,2},{3,67},{67,3},{4,68},{68... | collective-permute-start | bytes 6291464 | tf_op jit(solution)/shard_map/weight_gather/ppermute | solution.py:180
  78.5 49.0 %copy-start.1 = (bf16[1024,1024]{1,0:T(8,128)(2,1)S(1)}, bf16[1024,1024]{1,0:T(8,128)(2,1)}, u32[]{:S(2)}) copy-start(bf16[1024,1024]{1,0:T(8,128)(2,1)} %all-gather.2.cloned.1.call-done.weight.near) | copy-start | bytes 6291460
  106.2 1.0 copy-start.3
  107.4 11.9 %copy-start.11 = (f32[64,1024]{1,0:T(8,128)}, f32[64,1024]{1,0:T(8,128)S(1)}, u32[]{:S(2)}) copy-start(f32[64,1024]{1,0:T(8,128)S(1)} %get-tuple-element.19.raw) | copy-start | bytes 786436
  120.2 28.2 %collective-permute-start.7 = (bf16[4,64,1024]{2,1,0:T(8,128)(2,1)}, bf16[4,64,1024]{2,1,0:T(8,128)(2,1)}, u32[]{:S(2)}, u32[]{:S(2)}) collective-permute-start(bf16[4,64,1024]{2,1,0:T(8,128)(2,1)} %slice.8.rows), channel_id=1, source_target_pairs={{0,64},{64,0},{1,65},{65,1},{2,66},{66,2},{3,67},{67,3},{4,68},{68... | collective-permute-start | bytes 1572872 | tf_op jit(solution)/shard_map/refresh/ppermute | solution.py:206
  125.5 16.5 %collective-permute-start.6 = (f32[64,1024]{1,0:T(8,128)}, f32[64,1024]{1,0:T(8,128)S(1)}, u32[]{:S(2)}, u32[]{:S(2)}) collective-permute-start(f32[64,1024]{1,0:T(8,128)} %copy-done.11), channel_id=1, source_target_pairs={{0,64},{64,0},{1,65},{65,1},{2,66},{66,2},{3,67},{67,3},{4,68},{68... | collective-permute-start | bytes 786440 | tf_op jit(solution)/shard_map/refresh/ppermute | solution.py:202
  132.3 13.3 %copy-start.4 = (f32[2048,64]{0,1:T(8,128)S(1)}, f32[2048,64]{0,1:T(8,128)}, u32[]{:S(2)}) copy-start(f32[2048,64]{0,1:T(8,128)} %param.10) | copy-start | bytes 1572868
  133.2 25.9 %collective-permute-start.4 = (f32[256,256]{1,0:T(8,128)}, f32[256,256]{1,0:T(8,128)}, u32[]{:S(2)}, u32[]{:S(2)}) collective-permute-start(f32[256,256]{1,0:T(8,128)} %get-tuple-element.29), channel_id=1, source_target_pairs={{0,3},{1,0},{2,1},{3,2},{4,7},{5,4},{6,5},{7,6},{8,11},{9,8},{10,9... | collective-permute-start | bytes 786440 | tf_op jit(solution)/shard_map/values/ppermute | solution.py:226
  136.0 23.1 %collective-permute-start.3 = (f32[256,256]{1,0:T(8,128)}, f32[256,256]{1,0:T(8,128)}, u32[]{:S(2)}, u32[]{:S(2)}) collective-permute-start(f32[256,256]{1,0:T(8,128)} %get-tuple-element.30), channel_id=1, source_target_pairs={{0,2},{1,3},{2,0},{3,1},{4,6},{5,7},{6,4},{7,5},{8,10},{9,11},{10,... | collective-permute-start | bytes 786440 | tf_op jit(solution)/shard_map/values/ppermute | solution.py:226
  139.1 20.0 %collective-permute-start.2 = (f32[256,256]{1,0:T(8,128)}, f32[256,256]{1,0:T(8,128)}, u32[]{:S(2)}, u32[]{:S(2)}) collective-permute-start(f32[256,256]{1,0:T(8,128)} %get-tuple-element.28), channel_id=1, source_target_pairs={{0,1},{1,2},{2,3},{3,0},{4,5},{5,6},{6,7},{7,4},{8,9},{9,10},{10,1... | collective-permute-start | bytes 786440 | tf_op jit(solution)/shard_map/values/ppermute | solution.py:226
  142.7 5.8 %collective-permute-start.8 = (f32[64,256]{1,0:T(8,128)S(1)}, f32[64,256]{1,0:T(8,128)S(1)}, u32[]{:S(2)}, u32[]{:S(2)}) collective-permute-start(f32[64,256]{1,0:T(8,128)S(1)} %convert_reduce_fusion.part), channel_id=1, source_target_pairs={{0,64},{64,0},{1,65},{65,1},{2,66},{66,2},{3,67},{67,3},{4,68},{68... | collective-permute-start | bytes 196616 | tf_op jit(solution)/shard_map/refresh/ppermute | solution.py:207
  148.5 6.6 %copy-start.16 = (bf16[256,64]{1,0:T(8,128)(2,1)S(1)}, bf16[256,64]{1,0:T(8,128)(2,1)}, u32[]{:S(2)}) copy-start(bf16[256,64]{1,0:T(8,128)(2,1)} %copy-done.15) | copy-start | bytes 98308
  150.9 1.4 copy-start.10
  152.3 2.8 %copy-start.5 = (f32[2048,64]{0,1:T(8,128)S(1)}, f32[2048,64]{0,1:T(8,128)}, u32[]{:S(2)}) copy-start(f32[2048,64]{0,1:T(8,128)} %param.10) | copy-start | bytes 1572868
  152.3 2.8 %copy-start.7 = (bf16[256,1024]{1,0:T(8,128)(2,1)S(1)}, bf16[256,1024]{1,0:T(8,128)(2,1)}, u32[]{:S(2)}) copy-start(bf16[256,1024]{1,0:T(8,128)(2,1)} %cotangent.5) | copy-start | bytes 1572868
  (5 other events, 4.6 us)
Sparse Core Ops, SparseCore 0:
  17.4 55.5 all-gather.1

commit v2 on v1

--- a/solution.py
+++ b/solution.py
@@ -115,8 +115,11 @@
     fresh = (down[:, own] - down_learning_rate * normed(grad)).astype(bf16)
     up_grad = load_tiles(gathered, 8, 8).astype(bf16)
     for p in range(4):
-        out[p, :, :1024] = fresh
-        out[p, :, 1024:] = up_grad[:, 256 * p : 256 * p + 256]
+        out[p, :64, :] = fresh
+        for i in range(4):
+            out[p, 64:, 256 * i : 256 * i + 256] = up_grad[
+                16 * i : 16 * i + 16, 256 * p : 256 * p + 256
+            ]
 
 
 def down_kernel(core, raw, raw_other, down, out):
@@ -125,14 +128,21 @@
     out[:, other] = down[:, other] - down_learning_rate * normed(raw_other[...])
 
 
-def finish_kernel(core, place, rows, rows_other, part, part_other, up, scorer_ref, up_ref):
-    first = core[0] == 0
+def part_sum(rows):
+    wide = rows[0, 64:, :].astype(f32)
+    for p in range(1, 4):
+        wide = wide + rows[p, 64:, :].astype(f32)
+    return jnp.concatenate([wide[:, 256 * i : 256 * i + 256] for i in range(4)], axis=0)
+
+
+def finish_kernel(core, place, rows, rows_other, up, scorer_ref, up_ref):
+    own, other = halves(core[0], 1024)
     for p in range(4):
-        mine, theirs = rows[p], rows_other[p]
-        scorer_ref[2048 * p : 2048 * p + 1024, :] = jnp.where(first, mine, theirs).T
-        scorer_ref[2048 * p + 1024 : 2048 * p + 2048, :] = jnp.where(first, theirs, mine).T
+        scorer_ref[:, pl.ds(pl.multiple_of(2048 * p + own.start, 1024), 1024)] = rows[p, :64, :]
+        scorer_ref[:, pl.ds(pl.multiple_of(2048 * p + other.start, 1024), 1024)] = rows_other[p, :64, :]
     columns = pl.ds(pl.multiple_of(place[0] * 256, 256), 256)
-    up_ref[...] = up[:, columns] - up_learning_rate * normed(part[...] + part_other[...])
+    total = part_sum(rows) + part_sum(rows_other)
+    up_ref[...] = up[:, columns] - up_learning_rate * normed(total)
 
 
 def near_values_kernel(core, tokens, weight, rank, up, out):
@@ -143,11 +153,33 @@
     out[...] = dot(tokens[:, own], weight[...], NT) + adapter_scale * branch
 
 
-def far_values_kernel(core, tokens, weight, near, out):
+def far_values_kernel(core, place, tokens, weight, near, kept, *sent):
     _, other = halves(core[0], tokens.shape[1] // 2)
-    whole = near[...] + dot(tokens[:, other], weight[...], NT)
-    for p in range(4):
-        out[p] = whole[:, 256 * p : 256 * p + 256]
+    far_tokens = tokens[:, other]
+    for k, ref in enumerate((kept, *sent)):
+        first = pl.multiple_of(lax.rem(place[0] + k, 4) * 256, 256)
+        columns = pl.ds(first, 256)
+        ref[...] = near[:, columns] + dot(far_tokens, weight[columns, :], NT)
+
+
+def sum_values_kernel(*refs):
+    *parts, out = refs
+    out[...] = (parts[0][...] + parts[1][...] + parts[2][...] + parts[3][...]).astype(bf16)
+
+
+def tie_kernel(value, before, out):
+    del value, before, out
+
+
+def tie(value, before):
+    anywhere = pl.BlockSpec(memory_space=pl.ANY)
+    return pl.pallas_call(
+        tie_kernel,
+        out_shape=jax.ShapeDtypeStruct(value.shape, value.dtype),
+        in_specs=[anywhere, anywhere],
+        out_specs=anywhere,
+        input_output_aliases={0: 0},
+    )(value, before)
 
 
 def token_gradient_kernel(core, cotangent, near, far, back_low, down, out):
@@ -177,7 +209,6 @@
         )
     with jax.named_scope("weight_gather"):
         near = lax.all_gather(pair, "y", axis=0, tiled=True)
-        far = lax.ppermute(near, "c", swap)
 
     with jax.named_scope("gradients"):
         back_low, keep, send = call(
@@ -195,36 +226,41 @@
         parts = lax.all_to_all(parts, PLANE, 0, 0, tiled=True)
         total = call(total_kernel, shape(64, 16, 128), (), (parts,))
         gathered = lax.all_to_all(total, PLANE, 0, 0, tiled=True)
+    with jax.named_scope("weight_swap"):
+        near = tie(near, gathered)
+        far = lax.ppermute(near, "c", swap)
     with jax.named_scope("refresh"):
         rows, raw = call(
-            scorer_kernel, (shape(4, 64, 1280, dtype=bf16), shape(64, 1024)), (core,), (gathered, down)
+            scorer_kernel, (shape(4, 80, 1024, dtype=bf16), shape(64, 1024)), (core,), (gathered, down)
         )
         raw_other = lax.ppermute(raw, "c", swap)
         rows = lax.all_to_all(rows, "x", 0, 0, tiled=True)
-        part = jnp.sum(rows[:, :, 1024:].astype(f32), axis=0)
-        rows = rows[:, :, :1024]
         rows_other = lax.ppermute(rows, "c", swap)
-        part_other = lax.ppermute(part, "c", swap)
         refreshed_down = call(
             down_kernel, shape(64, 2048), (core,), (raw, raw_other, down)
         ).T
         scorer_a, refreshed_up = call(
             finish_kernel,
-            (shape(8192, 64, dtype=bf16), shape(64, 256)),
+            (shape(64, 8192, dtype=bf16), shape(64, 256)),
             (core, place),
-            (rows, rows_other, part, part_other, adapter_up),
-        )
+            (rows, rows_other, adapter_up),
+        )
+        scorer_a = scorer_a.T
     with jax.named_scope("values"):
         near_part = call(
             near_values_kernel, shape(256, 1024), (core,), (tokens, near, rank, adapter_up)
         )
-        whole = call(far_values_kernel, shape(4, 256, 256), (core,), (tokens, far, near_part))
-        at = lax.axis_index("x")
-        values = lax.dynamic_index_in_dim(whole, at, 0, keepdims=False)
-        for k in range(1, 4):
-            out = lax.dynamic_index_in_dim(whole, (at + k) % 4, 0, keepdims=False)
-            values = values + lax.ppermute(out, "x", [(i, (i + k) % 4) for i in range(4)])
-        values = values.astype(bf16)
+        kept, *sent = call(
+            far_values_kernel,
+            (shape(256, 256),) * 4,
+            (core, place),
+            (tokens, far, near_part),
+        )
+        came = [
+            lax.ppermute(part, "x", [(i, (i + k) % 4) for i in range(4)])
+            for k, part in enumerate(sent, 1)
+        ]
+        values = call(sum_values_kernel, shape(256, 256, dtype=bf16), (), (kept, *came))
     with jax.named_scope("grad_tokens"):
         grad_tokens = call(
             token_gradient_kernel,

time: 169 us -> 145 us (0.86)
  blocking collectives: 39.6 us -> 74.7 us
  waiting for transfers between devices: 35.1 us -> 5.02 us
  starting transfers between devices: 47.9 us -> 30.9 us
  local copies, waits for them, and re-layouts: 10.9 us -> 2.35 us
  other arithmetic: 6.24 us -> 2.61 us
    all_to_all x0 -> x1, blocking collectives: none -> 34.8 us  [body(): parts = lax.all_to_all(parts, PLANE, 0, 0, tiled=True)]
    all_gather x1, waiting for transfers between devices: 32.7 us -> 0.01 us  [body(): near = lax.all_gather(pair, 'y', axis=0, tiled=True)]
    all_to_all x1 -> x0, starting transfers between devices: 11.2 us -> none  [body(): parts = lax.all_to_all(parts, PLANE, 0, 0, tiled=True)]
    unnamed x37 -> x26, local copies, waits for them, and re-layouts: 8.89 us -> 2.14 us
    all_to_all x1, blocking collectives: 11.8 us -> 14.6 us  [body(): rows = lax.all_to_all(rows, 'x', 0, 0, tiled=True)]
    ppermute x4 -> x3, waiting for transfers between devices: 0.01 us -> 2.66 us  [body(): lax.ppermute(part, 'x', [(i, (i + k) % 4) for i in range(4)])]
    all_to_all x1, blocking collectives: 27.7 us -> 25.3 us  [body(): gathered = lax.all_to_all(total, PLANE, 0, 0, tiled=True)]
    ppermute x1, starting transfers between devices: 5.25 us -> 3.01 us  [body(): rows_other = lax.ppermute(rows, 'c', swap)]
  transfers between devices with their start and end apart: 11 -> 9, of which waited for: 2 -> 2; matrix products, arithmetic and copies ran while one was open for 4% -> 0% of each run, Pallas kernels for 8% -> 9%
where the time goes in v2:
time: 145 us; the launch traced here: 144 us
  blocking collectives  74.7 us (52%)
  starting transfers between devices  30.9 us (21%)
  Pallas kernels  14.4 us (10%)
  between operations  14.4 us (10%)
  waiting for transfers between devices  5.02 us (3%)
  other arithmetic  2.61 us (2%)
  local copies, waits for them, and re-layouts  2.35 us (2%)
    all_to_all x1, blocking collectives, body(): parts = lax.all_to_all(parts, PLANE, 0, 0, tiled=True)  34.8 us
    all_to_all x1, blocking collectives, body(): gathered = lax.all_to_all(total, PLANE, 0, 0, tiled=True)  25.3 us
    all_to_all x1, blocking collectives, body(): rows = lax.all_to_all(rows, 'x', 0, 0, tiled=True)  14.6 us
    pallas_call x10, Pallas kernels, call(): pl.pallas_call(kernel, out_shape=outs, in_specs=[pl.BlockSpec(memory_spac...  14.4 us
    ppermute x3, starting transfers between devices, body(): lax.ppermute(part, 'x', [(i, (i + k) % 4) for i in range(4)])  8.55 us
    ppermute x1, starting transfers between devices, body(): arrived = lax.ppermute(send, 'c', swap)  8.47 us
    ppermute x1, starting transfers between devices, body(): theirs = lax.ppermute(mine, 'zl', swap)  4.83 us
    ppermute x1, starting transfers between devices, body(): far = lax.ppermute(near, 'c', swap)  4.09 us
  transfers between devices with their start and end apart: 9, of which 2 were waited for; matrix products, arithmetic and copies ran while one was open for 0% of the time, Pallas kernels for 9%

profile of v2, /device:TPU:1, one launch (start us, length us, event | category | flops | bytes accessed | tf_op | source)
XLA Modules:
  0.0 144.3 jit_solution(7589123873815018911)
XLA Ops:
  7.3 0.8 convert_bitcast_fusion
  8.3 1.0 fusion
  9.3 4.8 %collective-permute-start = (bf16[64,1024]{1,0:T(8,128)(2,1)S(1)}, bf16[64,1024]{1,0:T(8,128)(2,1)S(1)}, u32[]{:S(2)}, u32[]{:S(2)}) collective-permute-start(bf16[64,1024]{1,0:T(8,128)(2,1)S(1)} %fusion), channel_id=1, source_target_pairs={{0,4},{4,0},{1,5},{5,1},{2,6},{6,2},{3,7},{7,3},{8,12},{12,8},{9,1... | collective-permute-start | bytes 393224 | tf_op jit(solution)/shard_map/dequant/ppermute | solution.py:205
  14.1 2.3 %collective-permute-done = bf16[64,1024]{1,0:T(8,128)(2,1)S(1)} collective-permute-done((bf16[64,1024]{1,0:T(8,128)(2,1)S(1)}, bf16[64,1024]{1,0:T(8,128)(2,1)S(1)}, u32[]{:S(2)}, u32[]{:S(2)}) %collective-permute-start) | collective-permute-done | bytes 131104 | tf_op jit(solution)/shard_map/dequant/ppermute | solution.py:205
  17.3 1.1 gradients.2
  18.4 8.5 %collective-permute-start.1 = (f32[64,8,128]{2,1,0:T(8,128)S(1)}, f32[64,8,128]{2,1,0:T(8,128)S(1)}, u32[]{:S(2)}, u32[]{:S(2)}) collective-permute-start(f32[64,8,128]{2,1,0:T(8,128)S(1)} %get-tuple-element.19), channel_id=1, source_target_pairs={{0,64},{64,0},{1,65},{65,1},{2,66},{66,2},{3,67},{67,3},{4,68},{68... | collective-permute-start | bytes 786440 | tf_op jit(solution)/shard_map/gradients/ppermute | solution.py:220
  26.9 1.2 gradients.3
  28.2 34.8 %all_to_all.15.parts = f32[64,16,128]{2,1,0:T(8,128)S(1)} all-to-all(f32[64,16,128]{2,1,0:T(8,128)S(1)} %pad_maximum_fusion), channel_id=1, replica_groups=mesh['zh'=4,'c'=2,'y'=8,'zl'=2,'x'=4] {'zh','y','zl'}, dimensions={0} | all-to-all | bytes 1048576 | tf_op jit(solution)/shard_map/plane_sum/all_to_all | solution.py:226
  63.1 25.3 %all_to_all.16.before.gathered = f32[64,16,128]{2,1,0:T(8,128)} all-to-all(f32[64,16,128]{2,1,0:T(8,128)S(1)} %plane_sum.1), channel_id=1, replica_groups=mesh['zh'=4,'c'=2,'y'=8,'zl'=2,'x'=4] {'zh','y','zl'}, dimensions={0} | all-to-all | bytes 1048576 | tf_op jit(solution)/shard_map/plane_sum/all_to_all | solution.py:228
  88.4 4.1 %collective-permute-start.2 = (bf16[1024,1024]{1,0:T(8,128)(2,1)}, bf16[1024,1024]{1,0:T(8,128)(2,1)}, u32[]{:S(2)}, u32[]{:S(2)}) collective-permute-start(bf16[1024,1024]{1,0:T(8,128)(2,1)} %weight_swap.1.weight.near), channel_id=1, source_target_pairs={{0,64},{64,0},{1,65},{65,1},{2,66},{66,2},{3,67},{67,3},{4,68},{68... | collective-permute-start | bytes 6291464 | tf_op jit(solution)/shard_map/weight_swap/ppermute | solution.py:231
  92.5 1.0 copy-done.3
  93.6 1.0 copy-done.5
  94.7 14.6 %all_to_all.17.rows = bf16[4,80,1024]{2,1,0:T(8,128)(2,1)} all-to-all(bf16[4,80,1024]{2,1,0:T(8,128)(2,1)S(1)} %get-tuple-element.28), channel_id=1, replica_groups=mesh['zh'=4,'c'=2,'y'=8,'zl'=2,'x'=4] {'x'}, dimensions={0} | all-to-all | bytes 1310720 | tf_op jit(solution)/shard_map/refresh/all_to_all | solution.py:237
  109.3 3.0 %collective-permute-start.7 = (bf16[4,80,1024]{2,1,0:T(8,128)(2,1)}, bf16[4,80,1024]{2,1,0:T(8,128)(2,1)}, u32[]{:S(2)}, u32[]{:S(2)}) collective-permute-start(bf16[4,80,1024]{2,1,0:T(8,128)(2,1)} %all_to_all.17.rows), channel_id=1, source_target_pairs={{0,64},{64,0},{1,65},{65,1},{2,66},{66,2},{3,67},{67,3},{4,68},{68... | collective-permute-start | bytes 1966088 | tf_op jit(solution)/shard_map/refresh/ppermute | solution.py:238
  112.3 1.9 %collective-permute-start.6 = (f32[64,1024]{1,0:T(8,128)}, f32[64,1024]{1,0:T(8,128)S(1)}, u32[]{:S(2)}, u32[]{:S(2)}) collective-permute-start(f32[64,1024]{1,0:T(8,128)} %copy-done.9), channel_id=1, source_target_pairs={{0,64},{64,0},{1,65},{65,1},{2,66},{66,2},{3,67},{67,3},{4,68},{68... | collective-permute-start | bytes 786440 | tf_op jit(solution)/shard_map/refresh/ppermute | solution.py:236
  114.2 1.5 %values.3.near = f32[256,1024]{1,0:T(8,128)S(1)} custom-call(s32[1]{0:T(128)} %bitcast.core, bf16[256,2048]{1,0:T(8,128)(2,1)S(1)} %copy-done.1, bf16[1024,1024]{1,0:T(8,128)(2,1)S(1)} %copy-done, f32[256,64]{1,0:T(8,128)S(1)} %get-tuple-element.21.rank, f32[64,1024]{1,0:T(8,128)S(1)} %copy-done.8), custom_call_target="tpu_custom_call" | custom-call | bytes 1048576 | tf_op jit(solution)/shard_map/values/pallas_call | solution.py:42
  115.8 2.4 %values.4 = (f32[256,256]{1,0:T(8,128)S(1)}, f32[256,256]{1,0:T(8,128)S(1)}, f32[256,256]{1,0:T(8,128)S(1)}, f32[256,256]{1,0:T(8,128)S(1)}) custom-call(s32[1]{0:T(128)} %bitcast.core, s32[1]{0:T(128)} %bitcast.1.place, bf16[256,2048]{1,0:T(8,128)(2,1)S(1)} %copy-done.1, bf16[1024,1024]{1,0:T(8,128)(2,1)} %collective-permute-done.2.weight.far, ...), custom_call_target="tpu_custom_call" | custom-call | bytes 1048576 | tf_op jit(solution)/shard_map/values/pallas_call | solution.py:42
  118.2 2.3 %collective-permute-start.3 = (f32[256,256]{1,0:T(8,128)S(1)}, f32[256,256]{1,0:T(8,128)S(1)}, u32[]{:S(2)}, u32[]{:S(2)}) collective-permute-start(f32[256,256]{1,0:T(8,128)S(1)} %get-tuple-element.23), channel_id=1, source_target_pairs={{0,1},{1,2},{2,3},{3,0},{4,5},{5,6},{6,7},{7,4},{8,9},{9,10},{10,1... | collective-permute-start | bytes 786440 | tf_op jit(solution)/shard_map/values/ppermute | solution.py:260
  120.6 3.7 %collective-permute-start.4 = (f32[256,256]{1,0:T(8,128)S(1)}, f32[256,256]{1,0:T(8,128)S(1)}, u32[]{:S(2)}, u32[]{:S(2)}) collective-permute-start(f32[256,256]{1,0:T(8,128)S(1)} %get-tuple-element.24), channel_id=1, source_target_pairs={{0,2},{1,3},{2,0},{3,1},{4,6},{5,7},{6,4},{7,5},{8,10},{9,11},{10,... | collective-permute-start | bytes 786440 | tf_op jit(solution)/shard_map/values/ppermute | solution.py:260
  124.3 2.5 %collective-permute-start.5 = (f32[256,256]{1,0:T(8,128)S(1)}, f32[256,256]{1,0:T(8,128)S(1)}, u32[]{:S(2)}, u32[]{:S(2)}) collective-permute-start(f32[256,256]{1,0:T(8,128)S(1)} %get-tuple-element.25), channel_id=1, source_target_pairs={{0,3},{1,0},{2,1},{3,2},{4,7},{5,4},{6,5},{7,6},{8,11},{9,8},{10,9... | collective-permute-start | bytes 786440 | tf_op jit(solution)/shard_map/values/ppermute | solution.py:260
  126.8 0.9 refresh.4
  127.7 2.3 %refresh.5 = (bf16[64,8192]{1,0:T(8,128)(2,1)}, f32[64,256]{1,0:T(8,128)}) custom-call(s32[1]{0:T(128)} %bitcast.core, s32[1]{0:T(128)} %bitcast.1.place, bf16[4,80,1024]{2,1,0:T(8,128)(2,1)} %all_to_all.17.rows, bf16[4,80,1024]{2,1,0:T(8,128)(2,1)} %collective-permute-done.7.rows_other, f32[64,1024]{1,0:T(8,128)S(1)} %copy-done.8), custom_call_target="tpu_custom_call" | custom-call | bytes 1048576 | tf_op jit(solution)/shard_map/refresh/pallas_call | solution.py:42
  130.1 4.1 %grad_tokens.1 = bf16[256,2048]{1,0:T(8,128)(2,1)} custom-call(s32[1]{0:T(128)} %bitcast.core, bf16[256,1024]{1,0:T(8,128)(2,1)S(1)} %copy-done.7, bf16[1024,1024]{1,0:T(8,128)(2,1)S(1)} %copy-done, bf16[1024,1024]{1,0:T(8,128)(2,1)} %collective-permute-done.2.weight.far, bf16[256,64]{1,0:T(8,128)(2,1)S(1)} %copy-done.12, f32[64,2048]{1,0:T(8,128)S(1)} %bitcast.17), custom_call_target="tpu_custom_call" | custom-call | bytes 1048576 | tf_op jit(solution)/shard_map/grad_tokens/pallas_call | solution.py:42
  134.1 2.7 %collective-permute-done.5.refs_3_ = f32[256,256]{1,0:T(8,128)S(1)} collective-permute-done((f32[256,256]{1,0:T(8,128)S(1)}, f32[256,256]{1,0:T(8,128)S(1)}, u32[]{:S(2)}, u32[]{:S(2)}) %collective-permute-start.5) | collective-permute-done | bytes 262176 | tf_op jit(solution)/shard_map/values/ppermute | solution.py:260
  (43 shorter events, 2.0 us)
Async XLA Ops:
  7.2 10.1 %copy-start.1 = (bf16[256,2048]{1,0:T(8,128)(2,1)S(1)}, bf16[256,2048]{1,0:T(8,128)(2,1)}, u32[]{:S(2)}) copy-start(bf16[256,2048]{1,0:T(8,128)(2,1)} %tokens.7) | copy-start | bytes 3145732
  7.2 10.1 %copy-start.6 = (bf16[256,1024]{1,0:T(8,128)(2,1)S(1)}, bf16[256,1024]{1,0:T(8,128)(2,1)}, u32[]{:S(2)}) copy-start(bf16[256,1024]{1,0:T(8,128)(2,1)} %cotangent.5) | copy-start | bytes 1572868
  7.2 10.1 %copy-start.8 = (f32[64,1024]{1,0:T(8,128)S(1)}, f32[64,1024]{1,0:T(8,128)}, u32[]{:S(2)}) copy-start(f32[64,1024]{1,0:T(8,128)} %up.5) | copy-start | bytes 786436
  7.2 19.7 %copy-start.2 = (f32[2048,64]{0,1:T(8,128)S(1)}, f32[2048,64]{0,1:T(8,128)}, u32[]{:S(2)}) copy-start(f32[2048,64]{0,1:T(8,128)} %param.10) | copy-start | bytes 1572868
  7.2 81.2 %all-gather.2.cloned.1.call-start = ((), (), s32[]{:S(2)}) async-start(), calls=%async_computation.3 | async-start | bytes 2359296 | tf_op jit(solution)/shard_map/weight_gather/all_gather | solution.py:211
  9.3 7.2 %collective-permute-start = (bf16[64,1024]{1,0:T(8,128)(2,1)S(1)}, bf16[64,1024]{1,0:T(8,128)(2,1)S(1)}, u32[]{:S(2)}, u32[]{:S(2)}) collective-permute-start(bf16[64,1024]{1,0:T(8,128)(2,1)S(1)} %fusion), channel_id=1, source_target_pairs={{0,4},{4,0},{1,5},{5,1},{2,6},{6,2},{3,7},{7,3},{8,12},{12,8},{9,1... | collective-permute-start | bytes 393224 | tf_op jit(solution)/shard_map/dequant/ppermute | solution.py:205
  18.4 9.8 %copy-start.11 = (bf16[256,64]{1,0:T(8,128)(2,1)}, bf16[256,64]{1,0:T(8,128)(2,1)S(1)}, u32[]{:S(2)}) copy-start(bf16[256,64]{1,0:T(8,128)(2,1)S(1)} %get-tuple-element.26.back_low) | copy-start | bytes 98308
  18.4 9.7 %collective-permute-start.1 = (f32[64,8,128]{2,1,0:T(8,128)S(1)}, f32[64,8,128]{2,1,0:T(8,128)S(1)}, u32[]{:S(2)}, u32[]{:S(2)}) collective-permute-start(f32[64,8,128]{2,1,0:T(8,128)S(1)} %get-tuple-element.19), channel_id=1, source_target_pairs={{0,64},{64,0},{1,65},{65,1},{2,66},{66,2},{3,67},{67,3},{4,68},{68... | collective-permute-start | bytes 786440 | tf_op jit(solution)/shard_map/gradients/ppermute | solution.py:220
  88.4 25.8 %copy-start = (bf16[1024,1024]{1,0:T(8,128)(2,1)S(1)}, bf16[1024,1024]{1,0:T(8,128)(2,1)}, u32[]{:S(2)}) copy-start(bf16[1024,1024]{1,0:T(8,128)(2,1)} %weight_swap.1.weight.near) | copy-start | bytes 6291460
  88.4 27.3 %collective-permute-start.2 = (bf16[1024,1024]{1,0:T(8,128)(2,1)}, bf16[1024,1024]{1,0:T(8,128)(2,1)}, u32[]{:S(2)}, u32[]{:S(2)}) collective-permute-start(bf16[1024,1024]{1,0:T(8,128)(2,1)} %weight_swap.1.weight.near), channel_id=1, source_target_pairs={{0,64},{64,0},{1,65},{65,1},{2,66},{66,2},{3,67},{67,3},{4,68},{68... | collective-permute-start | bytes 6291464 | tf_op jit(solution)/shard_map/weight_swap/ppermute | solution.py:231
  92.5 1.0 copy-start.3
  93.6 1.0 copy-start.5
  94.7 14.6 %copy-start.9 = (f32[64,1024]{1,0:T(8,128)}, f32[64,1024]{1,0:T(8,128)S(1)}, u32[]{:S(2)}) copy-start(f32[64,1024]{1,0:T(8,128)S(1)} %get-tuple-element.27.raw) | copy-start | bytes 786436
  109.3 18.5 %collective-permute-start.7 = (bf16[4,80,1024]{2,1,0:T(8,128)(2,1)}, bf16[4,80,1024]{2,1,0:T(8,128)(2,1)}, u32[]{:S(2)}, u32[]{:S(2)}) collective-permute-start(bf16[4,80,1024]{2,1,0:T(8,128)(2,1)} %all_to_all.17.rows), channel_id=1, source_target_pairs={{0,64},{64,0},{1,65},{65,1},{2,66},{66,2},{3,67},{67,3},{4,68},{68... | collective-permute-start | bytes 1966088 | tf_op jit(solution)/shard_map/refresh/ppermute | solution.py:238
  112.3 14.5 %collective-permute-start.6 = (f32[64,1024]{1,0:T(8,128)}, f32[64,1024]{1,0:T(8,128)S(1)}, u32[]{:S(2)}, u32[]{:S(2)}) collective-permute-start(f32[64,1024]{1,0:T(8,128)} %copy-done.9), channel_id=1, source_target_pairs={{0,64},{64,0},{1,65},{65,1},{2,66},{66,2},{3,67},{67,3},{4,68},{68... | collective-permute-start | bytes 786440 | tf_op jit(solution)/shard_map/refresh/ppermute | solution.py:236
  115.8 11.1 %copy-start.4 = (f32[2048,64]{0,1:T(8,128)S(1)}, f32[2048,64]{0,1:T(8,128)}, u32[]{:S(2)}) copy-start(f32[2048,64]{0,1:T(8,128)} %param.10) | copy-start | bytes 1572868
  115.8 11.0 %copy-start.10 = (f32[64,1024]{1,0:T(8,128)S(1)}, f32[64,1024]{1,0:T(8,128)}, u32[]{:S(2)}) copy-start(f32[64,1024]{1,0:T(8,128)} %copy-done.9) | copy-start | bytes 786436
  118.2 11.9 %copy-start.7 = (bf16[256,1024]{1,0:T(8,128)(2,1)S(1)}, bf16[256,1024]{1,0:T(8,128)(2,1)}, u32[]{:S(2)}) copy-start(bf16[256,1024]{1,0:T(8,128)(2,1)} %cotangent.5) | copy-start | bytes 1572868
  118.2 11.8 %copy-start.12 = (bf16[256,64]{1,0:T(8,128)(2,1)S(1)}, bf16[256,64]{1,0:T(8,128)(2,1)}, u32[]{:S(2)}) copy-start(bf16[256,64]{1,0:T(8,128)(2,1)} %copy-done.11) | copy-start | bytes 98308
  118.2 15.9 %collective-permute-start.3 = (f32[256,256]{1,0:T(8,128)S(1)}, f32[256,256]{1,0:T(8,128)S(1)}, u32[]{:S(2)}, u32[]{:S(2)}) collective-permute-start(f32[256,256]{1,0:T(8,128)S(1)} %get-tuple-element.23), channel_id=1, source_target_pairs={{0,1},{1,2},{2,3},{3,0},{4,5},{5,6},{6,7},{7,4},{8,9},{9,10},{10,1... | collective-permute-start | bytes 786440 | tf_op jit(solution)/shard_map/values/ppermute | solution.py:260
  120.6 13.6 %collective-permute-start.4 = (f32[256,256]{1,0:T(8,128)S(1)}, f32[256,256]{1,0:T(8,128)S(1)}, u32[]{:S(2)}, u32[]{:S(2)}) collective-permute-start(f32[256,256]{1,0:T(8,128)S(1)} %get-tuple-element.24), channel_id=1, source_target_pairs={{0,2},{1,3},{2,0},{3,1},{4,6},{5,7},{6,4},{7,5},{8,10},{9,11},{10,... | collective-permute-start | bytes 786440 | tf_op jit(solution)/shard_map/values/ppermute | solution.py:260
  124.3 12.5 %collective-permute-start.5 = (f32[256,256]{1,0:T(8,128)S(1)}, f32[256,256]{1,0:T(8,128)S(1)}, u32[]{:S(2)}, u32[]{:S(2)}) collective-permute-start(f32[256,256]{1,0:T(8,128)S(1)} %get-tuple-element.25), channel_id=1, source_target_pairs={{0,3},{1,0},{2,1},{3,2},{4,7},{5,4},{6,5},{7,6},{8,11},{9,8},{10,9... | collective-permute-start | bytes 786440 | tf_op jit(solution)/shard_map/values/ppermute | solution.py:260
Sparse Core Ops, SparseCore 0:
  17.4 57.7 all-gather.1

commit v3 on v2

v3 whole, which is shorter than its diff:
```python
import math

import jax
import jax.numpy as jnp
from jax import lax
from jax.experimental import pallas as pl
from jax.experimental.pallas import tpu as pltpu
from jax.sharding import Mesh
from jax.sharding import PartitionSpec as P

MODEL_WIDTH = 8192
QB = 128
INV_ROOT = 1.0 / math.sqrt(MODEL_WIDTH)

adapter_scale = 0.25
down_learning_rate = 1.0
up_learning_rate = 0.1
eps_norm = 1e-06

f32 = jnp.float32
bf16 = jnp.bfloat16
PLANE = ("zh", "y", "zl")
LIMIT = 32 * 1024 * 1024
WHOLE = 60 * 1024 * 1024

NN = (((1,), (0,)), ((), ()))
NT = (((1,), (1,)), ((), ()))
TN = (((0,), (0,)), ((), ()))


def dot(a, b, dims):
    return lax.dot_general(a, b, dims, preferred_element_type=f32)


def thirds(a):
    high = a.astype(bf16)
    rest = a - high.astype(f32)
    middle = rest.astype(bf16)
    return high, middle, (rest - middle.astype(f32)).astype(bf16)


def load(sources, places, sems):
    copies = [pltpu.make_async_copy(a, b, sems.at[i]) for i, (a, b) in enumerate(zip(sources, places))]
    for copy in copies:
        copy.start()
    for copy in copies:
        copy.wait()


def cost(mib):
    return pl.CostEstimate(flops=0, bytes_accessed=mib << 20, transcendentals=0)


def call(kernel, outs, scalars, stored, arrays, limit=LIMIT, after=()):
    first = len(scalars)
    count = len(stored)
    last = first + count + len(arrays)

    def loaded(*refs):
        refs = refs[:last] + refs[last + len(after) :]
        sources, others = refs[first : first + count], refs[first + count :]
        if count:
            *others, sems = others
            places = others[len(others) - count :]
            load(sources, places, sems)
            others = others[: len(others) - count]
            kernel(*refs[:first], *places, *others)
        else:
            kernel(*refs)

    scratch = [pltpu.VMEM(a.shape, a.dtype) for a in stored]
    return pl.pallas_call(
        loaded,
        out_shape=outs,
        in_specs=[pl.BlockSpec(memory_space=pltpu.SMEM)] * first
        + [pl.BlockSpec(memory_space=pltpu.HBM)] * count
        + [pl.BlockSpec(memory_space=pltpu.VMEM)] * len(arrays)
        + [pl.BlockSpec(memory_space=pl.ANY)] * len(after),
        out_specs=jax.tree.map(lambda _: pl.BlockSpec(memory_space=pltpu.VMEM), outs),
        scratch_shapes=scratch + [pltpu.SemaphoreType.DMA((count,))] * (count > 0),
        compiler_params=pltpu.CompilerParams(vmem_limit_bytes=limit),
        cost_estimate=cost(4),
    )(*scalars, *stored, *arrays, *after)


def shape(*dims, dtype=f32):
    return jax.ShapeDtypeStruct(dims, dtype)


def halves(core, width):
    first = pl.multiple_of(core * width, width)
    return pl.ds(first, width), pl.ds(pl.multiple_of(width - first, width), width)


def store_tiles(ref, wide, first):
    rows, columns = wide.shape[0] // 8, wide.shape[1] // 128
    for i in range(rows):
        for j in range(columns):
            ref[i * columns + j, first : first + 8] = wide[
                8 * i : 8 * i + 8, 128 * j : 128 * j + 128
            ]


def load_tiles(ref):
    halves_of = [ref[i].astype(f32) for i in range(64)]
    return [
        jnp.concatenate(
            [
                jnp.concatenate([halves_of[8 * i + j][first : first + 8] for j in range(8)], axis=1)
                for i in range(8)
            ],
            axis=0,
        )
        for first in (0, 8)
    ]


def dequant_kernel(core, codes, scales, out):
    wide = scales[...].astype(f32).T
    count = wide.shape[1] // 2
    mine = jnp.where(core[0] == 0, wide[:, :count], wide[:, count:])
    own, _ = halves(core[0], codes.shape[1] // 2)
    for j in range(count):
        block = codes[:, pl.ds(pl.multiple_of(own.start + QB * j, QB), QB)].astype(f32)
        out[:, QB * j : QB * j + QB] = (block * mine[:, j : j + 1]).astype(bf16)


def pair_kernel(low_first, mine, theirs, out):
    count = mine.shape[0]
    first = low_first[0] == 0
    out[:count] = jnp.where(first, mine[...], theirs[...])
    out[count:] = jnp.where(first, theirs[...], mine[...])


def gradients_kernel(
    core, tokens, cotangent, down, up, low_ref, rank_ref, send_ref, parts_ref, mark_ref
):
    mark_ref[...] = jnp.zeros(mark_ref.shape, f32)
    wide = cotangent[...]
    high, middle, low = thirds(up[...])
    back = dot(wide, low, NT) + dot(wide, middle, NT) + dot(wide, high, NT)
    back_low = (adapter_scale * back).astype(bf16)
    low_ref[...] = back_low
    own, other = halves(core[0], tokens.shape[1] // 2)
    store_tiles(send_ref, dot(back_low, tokens[:, other], TN) * INV_ROOT, 0)
    store_tiles(parts_ref, dot(back_low, tokens[:, own], TN) * INV_ROOT, 0)
    rank = dot(tokens[...], down[...].astype(bf16), NT) * INV_ROOT
    rank_ref[...] = rank
    high, middle, low = thirds(rank)
    up_grad = dot(low, wide, TN) + dot(middle, wide, TN) + dot(high, wide, TN)
    store_tiles(parts_ref, adapter_scale * up_grad, 8)


def parts_kernel(parts, arrived, out):
    for i in range(out.shape[0]):
        both = jnp.concatenate([parts[i, :8] + arrived[i], parts[i, 8:]], axis=0)
        out[i] = both.astype(bf16)


def total_kernel(parts, out):
    total = parts[0].astype(f32)
    for i in range(1, parts.shape[0]):
        total = total + parts[i].astype(f32)
    low = total.astype(bf16)
    for i in range(parts.shape[0]):
        out[i] = low


def normed(grad):
    mean = jnp.mean(grad * grad, axis=0, keepdims=True)
    return grad * lax.rsqrt(mean + eps_norm)


def scorer_kernel(core, weight, down, gathered, out, raw_ref, same):
    del weight, same
    own, _ = halves(core[0], down.shape[1] // 2)
    grad, up_grad = load_tiles(gathered)
    raw_ref[...] = grad.astype(bf16)
    fresh = (down[:, own] - down_learning_rate * normed(grad)).astype(bf16)
    up_grad = up_grad.astype(bf16)
    for p in range(4):
        out[p, :64, :] = fresh
        for i in range(4):
            out[p, 64:, 256 * i : 256 * i + 256] = up_grad[
                16 * i : 16 * i + 16, 256 * p : 256 * p + 256
            ]


def scorer_rows(core, weight, down, gathered):
    stored, here = pl.BlockSpec(memory_space=pltpu.HBM), pl.BlockSpec(memory_space=pltpu.VMEM)
    return pl.pallas_call(
        scorer_kernel,
        out_shape=(
            shape(4, 80, 1024, dtype=bf16),
            shape(64, 1024, dtype=bf16),
            shape(*weight.shape, dtype=bf16),
        ),
        in_specs=[pl.BlockSpec(memory_space=pltpu.SMEM), stored, here, here],
        out_specs=(here, here, stored),
        input_output_aliases={1: 2},
        compiler_params=pltpu.CompilerParams(vmem_limit_bytes=LIMIT),
        cost_estimate=cost(4),
    )(core, weight, down, gathered)


def down_kernel(core, down, raw, raw_other, out, mark_ref):
    mark_ref[...] = jnp.zeros(mark_ref.shape, f32)
    own, other = halves(core[0], down.shape[1] // 2)
    out[:, own] = down[:, own] - down_learning_rate * normed(raw[...].astype(f32))
    out[:, other] = down[:, other] - down_learning_rate * normed(raw_other[...].astype(f32))


def part_sum(rows):
    wide = rows[0, 64:80, :].astype(f32)
    for p in range(1, 4):
        wide = wide + rows[p, 64:80, :].astype(f32)
    return jnp.concatenate([wide[:, 256 * i : 256 * i + 256] for i in range(4)], axis=0)


def finish_kernel(core, place, up, rows, rows_other, scorer_ref, up_ref):
    own, other = halves(core[0], 1024)
    for p in range(4):
        scorer_ref[:, pl.ds(pl.multiple_of(2048 * p + own.start, 1024), 1024)] = rows[p, :64, :]
        scorer_ref[:, pl.ds(pl.multiple_of(2048 * p + other.start, 1024), 1024)] = rows_other[p, :64, :]
    columns = pl.ds(pl.multiple_of(place[0] * 256, 256), 256)
    total = part_sum(rows) + part_sum(rows_other)
    up_ref[...] = up[:, columns] - up_learning_rate * normed(total)


def near_values_kernel(core, tokens, weight, rank, up, out):
    own, _ = halves(core[0], tokens.shape[1] // 2)
    branch = lax.dot_general(
        rank[...], up[...], NN, precision=lax.Precision.HIGHEST, preferred_element_type=f32
    )
    out[...] = dot(tokens[:, own], weight[...], NT) + adapter_scale * branch


def far_values_kernel(core, tokens, weight, near, rows, out, *scratch):
    *places, result, sems, sem = scratch
    _, other = halves(core[0], tokens.shape[1] // 2)
    load((tokens.at[:, other], weight, near, rows), places, sems)
    tokens_at, weight_at, near_at, rows_at = places
    low = (near_at[...] + dot(tokens_at[...], weight_at[...], NT)).astype(bf16)
    for p in range(4):
        result[p, :80, :] = rows_at[p]
        for i in range(4):
            result[p, 80:, 256 * i : 256 * i + 256] = low[64 * i : 64 * i + 64, 256 * p : 256 * p + 256]
    copy = pltpu.make_async_copy(result, out, sem)
    copy.start()
    copy.wait()


def far_values(core, tokens, weight, near, rows):
    stored = pl.BlockSpec(memory_space=pltpu.HBM)
    out = (rows.shape[0], rows.shape[1] + 64, rows.shape[2])
    return pl.pallas_call(
        far_values_kernel,
        out_shape=shape(*out, dtype=bf16),
        in_specs=[pl.BlockSpec(memory_space=pltpu.SMEM)] + [stored] * 4,
        out_specs=stored,
        scratch_shapes=[
            pltpu.VMEM((tokens.shape[0], tokens.shape[1] // 2), bf16),
            pltpu.VMEM(weight.shape, bf16),
            pltpu.VMEM(near.shape, f32),
            pltpu.VMEM(rows.shape, bf16),
            pltpu.VMEM(out, bf16),
            pltpu.SemaphoreType.DMA((4,)),
            pltpu.SemaphoreType.DMA,
        ],
        compiler_params=pltpu.CompilerParams(vmem_limit_bytes=WHOLE),
        cost_estimate=cost(8),
    )(core, tokens, weight, near, rows)


def sum_values_kernel(came, mark_1, mark_2, out, same):
    del mark_1, mark_2, same
    for i in range(4):
        total = came[0, 80:, 256 * i : 256 * i + 256].astype(f32)
        for p in range(1, 4):
            total = total + came[p, 80:, 256 * i : 256 * i + 256].astype(f32)
        out[64 * i : 64 * i + 64, :] = total.astype(bf16)


def sum_values(came, mark_1, mark_2):
    here, anywhere = pl.BlockSpec(memory_space=pltpu.VMEM), pl.BlockSpec(memory_space=pl.ANY)
    return pl.pallas_call(
        sum_values_kernel,
        out_shape=(shape(256, 256, dtype=bf16), shape(*came.shape, dtype=bf16)),
        in_specs=[here, anywhere, anywhere],
        out_specs=(here, here),
        input_output_aliases={0: 1},
        compiler_params=pltpu.CompilerParams(vmem_limit_bytes=LIMIT),
        cost_estimate=cost(4),
    )(came, mark_1, mark_2)


def token_gradients_kernel(core, cotangent, low, down, near, far, out, mark_ref, *scratch):
    mark_ref[...] = jnp.zeros(mark_ref.shape, f32)
    wide, thin, master, matrices, result, sems, out_sems = scratch
    width = matrices.shape[2]
    sources = (cotangent, low, down, near, far)
    places = (wide, thin, master, matrices.at[0], matrices.at[1])
    loads = [pltpu.make_async_copy(a, b, sems.at[i]) for i, (a, b) in enumerate(zip(sources, places))]
    for copy in loads:
        copy.start()
    for copy in loads[:3]:
        copy.wait()
    stores = []
    for h, place in enumerate(halves(core[0], width)):
        loads[3 + h].wait()
        for q in range(2):
            step = width // 2
            columns = pl.ds(pl.multiple_of(place.start + step * q, step), step)
            part = pl.ds(step * q, step)
            beside = dot(thin[...], master[:, columns].astype(bf16), NN) * INV_ROOT
            result[h, :, part] = (dot(wide[...], matrices[h, :, part], NN) + beside).astype(bf16)
            stores.append(
                pltpu.make_async_copy(
                    result.at[h, :, part], out.at[:, columns], out_sems.at[2 * h + q]
                )
            )
            stores[-1].start()
    for copy in stores:
        copy.wait()


def token_gradients(core, cotangent, low, down, near, far):
    rows, columns = cotangent.shape[0], down.shape[1]
    stored = pl.BlockSpec(memory_space=pltpu.HBM)
    return pl.pallas_call(
        token_gradients_kernel,
        out_shape=(shape(rows, columns, dtype=bf16), shape(8, 128)),
        in_specs=[pl.BlockSpec(memory_space=pltpu.SMEM)] + [stored] * 5,
        out_specs=(stored, pl.BlockSpec(memory_space=pltpu.VMEM)),
        scratch_shapes=[
            pltpu.VMEM(cotangent.shape, bf16),
            pltpu.VMEM(low.shape, bf16),
            pltpu.VMEM(down.shape, f32),
            pltpu.VMEM((2, *near.shape), bf16),
            pltpu.VMEM((2, rows, columns // 2), bf16),
            pltpu.SemaphoreType.DMA((5,)),
            pltpu.SemaphoreType.DMA((4,)),
        ],
        compiler_params=pltpu.CompilerParams(vmem_limit_bytes=WHOLE),
        cost_estimate=cost(8),
    )(core, cotangent, low, down, near, far)


def body(tokens, cotangent, codes, scales, adapter_down, adapter_up):
    core_at = lax.axis_index("c")
    core = core_at.astype(jnp.int32).reshape(1)
    place = lax.axis_index("x").astype(jnp.int32).reshape(1)
    down = adapter_down.T
    swap = [(0, 1), (1, 0)]
    half = codes.shape[0] // 2

    mark = shape(8, 128)
    z_low = lax.axis_index("zl").astype(jnp.int32).reshape(1)

    with jax.named_scope("dequant"):
        mine = call(
            dequant_kernel,
            shape(codes.shape[1], half, dtype=bf16),
            (core,),
            (codes.T, scales),
            (),
            WHOLE,
        )
        theirs = lax.ppermute(mine, "zl", swap)
    with jax.named_scope("gradients"):
        back_low, rank, send, parts, begun = call(
            gradients_kernel,
            (
                shape(256, 64, dtype=bf16),
                shape(256, 64),
                shape(64, 8, 128),
                shape(64, 16, 128),
                mark,
            ),
            (core,),
            (tokens, cotangent, down, adapter_up),
            (),
            WHOLE,
        )
        arrived = lax.ppermute(send, "c", swap)
    with jax.named_scope("weight_gather"):
        pair = call(
            pair_kernel,
            shape(128, half, dtype=bf16),
            (z_low,),
            (),
            (mine, theirs),
            after=(begun,),
        )
        weight = lax.all_gather(pair, "y", axis=0, tiled=True)
    with jax.named_scope("plane_sum"):
        parts = call(parts_kernel, shape(64, 16, 128, dtype=bf16), (), (), (parts, arrived))
        parts = lax.all_to_all(parts, PLANE, 0, 0, tiled=True)
        total = call(total_kernel, shape(64, 16, 128, dtype=bf16), (), (), (parts,))
        gathered = lax.all_to_all(total, PLANE, 0, 0, tiled=True)
    with jax.named_scope("weight_swap"):
        rows, raw, near = scorer_rows(core, weight, down, gathered)
        far = lax.ppermute(near, "c", swap)
        raw_other = lax.ppermute(raw, "c", swap)
    with jax.named_scope("values"):
        near_part = call(
            near_values_kernel, shape(256, 1024), (core,), (tokens, near, rank, adapter_up), (), WHOLE
        )
        sent = far_values(core, tokens, far, near_part, rows)
        came = lax.all_to_all(sent, "x", 0, 0, tiled=True)
    with jax.named_scope("refresh"):
        refreshed_down, refreshed = call(
            down_kernel, (shape(64, 2048), mark), (core,), (), (down, raw, raw_other)
        )
        refreshed_down = refreshed_down.T
    with jax.named_scope("grad_tokens"):
        grad_tokens, turned = token_gradients(core, cotangent, back_low, down, near, far)
    with jax.named_scope("values"):
        values, came = sum_values(came, turned, refreshed)
    with jax.named_scope("refresh"):
        came_other = lax.ppermute(came, "c", swap)
        scorer_a, refreshed_up = call(
            finish_kernel,
            (shape(64, 8192, dtype=bf16), shape(64, 256)),
            (core, place),
            (),
            (adapter_up, came, came_other),
        )
        scorer_a = scorer_a.T
    return (values, grad_tokens, refreshed_down, scorer_a, refreshed_up)


def solution(mesh):
    fine = Mesh(mesh.devices.reshape(4, 2, 8, 2, 4), ("zh", "c", "y", "zl", "x"))
    tokens_at = ("zh", "c", "y", "zl")
    in_specs = (
        P(tokens_at, "x"),
        P(tokens_at, None),
        P("x", ("y", "zl")),
        P("x", ("y", "zl")),
        P("x", None),
        P(),
    )
    out_specs = (
        P(tokens_at, "x"),
        P(tokens_at, "x"),
        P("x", None),
        P(),
        P(None, "x"),
    )
    return jax.shard_map(body, mesh=fine, in_specs=in_specs, out_specs=out_specs, check_vma=False)
```

time: 145 us -> 127 us (0.88)
  blocking collectives: 74.7 us -> 47.1 us
  Pallas kernels: 14.4 us -> 23.7 us
  waiting for transfers between devices: 5.02 us -> 12.1 us
  starting transfers between devices: 30.9 us -> 25.9 us
  other arithmetic: 2.61 us -> 0 us
    all_to_all x1 -> x0, blocking collectives: 14.6 us -> none  [body(): rows = lax.all_to_all(rows, 'x', 0, 0, tiled=True)]
    pallas_call x11 -> x12, Pallas kernels: 14.4 us -> 23.7 us  [the longest x8 13.9 us: call(): pl.pallas_call(loaded, out_shape=outs, in_specs=[pl.BlockSpec(memory_spac...]
    ppermute x4 -> x1, starting transfers between devices: 11.6 us -> 3 us  [body(): came_other = lax.ppermute(came, 'c', swap)]
    all_to_all x1, blocking collectives: 34.8 us -> 27.5 us  [body(): parts = lax.all_to_all(parts, PLANE, 0, 0, tiled=True)]
    all_to_all x0 -> x1, waiting for transfers between devices: none -> 7.24 us  [body(): came = lax.all_to_all(sent, 'x', 0, 0, tiled=True)]
    all_to_all x1, blocking collectives: 25.3 us -> 19.7 us  [body(): gathered = lax.all_to_all(total, PLANE, 0, 0, tiled=True)]
    all_to_all x0 -> x1, starting transfers between devices: none -> 4.04 us  [body(): came = lax.all_to_all(sent, 'x', 0, 0, tiled=True)]
    ppermute x1, waiting for transfers between devices: 2.34 us -> 0.01 us  [body(): theirs = lax.ppermute(mine, 'zl', swap)]
  transfers between devices with their start and end apart: 9 -> 7, of which waited for: 2 -> 4; matrix products, arithmetic and copies ran while one was open for 0% -> 0% of each run, Pallas kernels for 9% -> 12%
where the time goes in v3:
time: 127 us; the launch traced here: 126 us
  blocking collectives  47.1 us (37%)
  starting transfers between devices  25.9 us (20%)
  Pallas kernels  23.7 us (19%)
  between operations  14.2 us (11%)
  waiting for transfers between devices  12.1 us (10%)
  local copies, waits for them, and re-layouts  3.26 us (3%)
    all_to_all x1, blocking collectives, body(): parts = lax.all_to_all(parts, PLANE, 0, 0, tiled=True)  27.5 us
    all_to_all x1, blocking collectives, body(): gathered = lax.all_to_all(total, PLANE, 0, 0, tiled=True)  19.7 us
    pallas_call x8, Pallas kernels, call(): pl.pallas_call(loaded, out_shape=outs, in_specs=[pl.BlockSpec(memory_spac...  13.9 us
    all_to_all x1, waiting for transfers between devices, body(): came = lax.all_to_all(sent, 'x', 0, 0, tiled=True)  7.24 us
    ppermute x1, starting transfers between devices, body(): arrived = lax.ppermute(send, 'c', swap)  6.21 us
    ppermute x1, starting transfers between devices, body(): far = lax.ppermute(near, 'c', swap)  5.57 us
    pallas_call x1, Pallas kernels, token_gradients(): pl.pallas_call(token_gradients_kernel, out_shape=(shape(rows, columns, dt...  4.97 us
    ppermute x1, starting transfers between devices, body(): theirs = lax.ppermute(mine, 'zl', swap)  4.83 us
  transfers between devices with their start and end apart: 7, of which 4 were waited for; matrix products, arithmetic and copies ran while one was open for 0% of the time, Pallas kernels for 12%

profile of v3, /device:TPU:1, one launch (start us, length us, event | category | flops | bytes accessed | tf_op | source)
XLA Modules:
  0.0 126.3 jit_solution(17628881906624286437)
XLA Ops:
  7.2 1.9 %dequant.1.refs_1_ = bf16[64,1024]{1,0:T(8,128)(2,1)} custom-call(s32[1]{0:T(128)} %bitcast.refs_0_.core, bf16[64,2048]{1,0:T(8,128)(2,1)} %bitcast.11, bf16[16,64]{1,0:T(8,128)(2,1)} %refs_2_.3), custom_call_target="tpu_custom_call" | custom-call | bytes 4194304 | tf_op jit(solution)/shard_map/dequant/pallas_call | solution.py:72
  9.1 4.8 %collective-permute-start = (bf16[64,1024]{1,0:T(8,128)(2,1)}, bf16[64,1024]{1,0:T(8,128)(2,1)S(1)}, u32[]{:S(2)}, u32[]{:S(2)}) collective-permute-start(bf16[64,1024]{1,0:T(8,128)(2,1)} %dequant.1.refs_1_), channel_id=1, source_target_pairs={{0,4},{4,0},{1,5},{5,1},{2,6},{6,2},{3,7},{7,3},{8,12},{12,8},{9,1... | collective-permute-start | bytes 393224 | tf_op jit(solution)/shard_map/dequant/ppermute | solution.py:369
  14.0 4.8 %gradients.1 = (bf16[256,64]{1,0:T(8,128)(2,1)}, f32[256,64]{1,0:T(8,128)}, f32[64,8,128]{2,1,0:T(8,128)}, f32[64,16,128]{2,1,0:T(8,128)}, f32[8,128]{1,0:T(8,128)}) custom-call(s32[1]{0:T(128)} %bitcast.refs_0_.core, bf16[256,2048]{1,0:T(8,128)(2,1)} %tokens.1, bf16[256,1024]{1,0:T(8,128)(2,1)} %cotangent.1, f32[64,2048]{1,0:T(8,128)} %bitcast.7, ...), custom_call_target="tpu_custom_call" | custom-call | bytes 4194304 | tf_op jit(solution)/shard_map/gradients/pallas_call | solution.py:72
  19.5 0.7 weight_gather.1
  20.2 6.2 %collective-permute-start.1 = (f32[64,8,128]{2,1,0:T(8,128)}, f32[64,8,128]{2,1,0:T(8,128)S(1)}, u32[]{:S(2)}, u32[]{:S(2)}) collective-permute-start(f32[64,8,128]{2,1,0:T(8,128)} %get-tuple-element.23), channel_id=1, source_target_pairs={{0,64},{64,0},{1,65},{65,1},{2,66},{66,2},{3,67},{67,3},{4,68},{68... | collective-permute-start | bytes 786440 | tf_op jit(solution)/shard_map/gradients/ppermute | solution.py:385
  26.4 1.4 %collective-permute-done.1.refs_1_ = f32[64,8,128]{2,1,0:T(8,128)S(1)} collective-permute-done((f32[64,8,128]{2,1,0:T(8,128)}, f32[64,8,128]{2,1,0:T(8,128)S(1)}, u32[]{:S(2)}, u32[]{:S(2)}) %collective-permute-start.1) | collective-permute-done | bytes 262176 | tf_op jit(solution)/shard_map/gradients/ppermute | solution.py:385
  27.8 1.0 copy-done.4
  28.9 27.5 %all_to_all.15.refs_0_ = bf16[64,16,128]{2,1,0:T(8,128)(2,1)S(1)} all-to-all(bf16[64,16,128]{2,1,0:T(8,128)(2,1)S(1)} %plane_sum.2), channel_id=1, replica_groups=mesh['zh'=4,'c'=2,'y'=8,'zl'=2,'x'=4] {'zh','y','zl'}, dimensions={0} | all-to-all | bytes 524288 | tf_op jit(solution)/shard_map/plane_sum/all_to_all | solution.py:398
  56.4 19.7 %all_to_all.16.gathered = bf16[64,16,128]{2,1,0:T(8,128)(2,1)S(1)} all-to-all(bf16[64,16,128]{2,1,0:T(8,128)(2,1)S(1)} %plane_sum.3), channel_id=1, replica_groups=mesh['zh'=4,'c'=2,'y'=8,'zl'=2,'x'=4] {'zh','y','zl'}, dimensions={0} | all-to-all | bytes 524288 | tf_op jit(solution)/shard_map/plane_sum/all_to_all | solution.py:400
  76.2 0.8 copy-done.2
  77.0 5.6 %collective-permute-start.2 = (bf16[1024,1024]{1,0:T(8,128)(2,1)}, bf16[1024,1024]{1,0:T(8,128)(2,1)}, u32[]{:S(2)}, u32[]{:S(2)}) collective-permute-start(bf16[1024,1024]{1,0:T(8,128)(2,1)} %get-tuple-element.24.refs_2_.near), channel_id=1, source_target_pairs={{0,64},{64,0},{1,65},{65,1},{2,66},{66,2},{3,67},{67,3},{4,68},{68... | collective-permute-start | bytes 6291464 | tf_op jit(solution)/shard_map/weight_swap/ppermute | solution.py:403
  82.6 4.4 %values.3.near = f32[256,1024]{1,0:T(8,128)} custom-call(s32[1]{0:T(128)} %bitcast.refs_0_.core, bf16[256,2048]{1,0:T(8,128)(2,1)} %tokens.1, bf16[1024,1024]{1,0:T(8,128)(2,1)} %get-tuple-element.24.refs_2_.near, f32[256,64]{1,0:T(8,128)} %get-tuple-element.25.refs_3_, f32[64,1024]{1,0:T(8,128)} %refs_2_.5), custom_call_target="tpu_custom_call" | custom-call | bytes 4194304 | tf_op jit(solution)/shard_map/values/pallas_call | solution.py:72
  87.1 4.0 %values.4 = bf16[4,144,1024]{2,1,0:T(8,128)(2,1)} custom-call(s32[1]{0:T(128)} %bitcast.refs_0_.core, bf16[256,2048]{1,0:T(8,128)(2,1)} %tokens.1, bf16[1024,1024]{1,0:T(8,128)(2,1)} %collective-permute-done.2.weight.far, f32[256,1024]{1,0:T(8,128)} %values.3.near, bf16[4,80,1024]{2,1,0:T(8,128)(2,1)} %copy-done.2), custom_call_target="tpu_custom_call" | custom-call | bytes 8388608 | tf_op jit(solution)/shard_map/values/pallas_call | solution.py:256
  91.1 4.0 %all-to-all-start.2 = ((bf16[4,144,1024]{2,1,0:T(8,128)(2,1)}), bf16[4,144,1024]{2,1,0:T(8,128)(2,1)S(1)}, u32[]{:S(2)}, u32[]{:S(2)}) async-start(bf16[4,144,1024]{2,1,0:T(8,128)(2,1)} %values.4), calls=%async_computation.2 | async-start | bytes 2359296 | tf_op jit(solution)/shard_map/values/all_to_all | solution.py:410
  95.2 2.2 %collective-permute-start.3 = (bf16[64,1024]{1,0:T(8,128)(2,1)S(1)}, bf16[64,1024]{1,0:T(8,128)(2,1)S(1)}, u32[]{:S(2)}, u32[]{:S(2)}) collective-permute-start(bf16[64,1024]{1,0:T(8,128)(2,1)S(1)} %get-tuple-element.29.refs_2_), channel_id=1, source_target_pairs={{0,64},{64,0},{1,65},{65,1},{2,66},{66,2},{3,67},{67,3},{4,68},{68... | collective-permute-start | bytes 393224 | tf_op jit(solution)/shard_map/weight_swap/ppermute | solution.py:404
  97.3 1.0 collective-permute-done.3.refs_3_
  98.4 0.9 refresh.2
  99.3 5.0 %grad_tokens.1 = (bf16[256,2048]{1,0:T(8,128)(2,1)}, f32[8,128]{1,0:T(8,128)}) custom-call(s32[1]{0:T(128)} %bitcast.refs_0_.core, bf16[256,1024]{1,0:T(8,128)(2,1)} %cotangent.1, bf16[256,64]{1,0:T(8,128)(2,1)} %get-tuple-element.27.low, f32[64,2048]{1,0:T(8,128)} %bitcast.8, bf16[1024,1024]{1,0:T(8,128)(2,1)} %get-tuple-element.24.refs_2_.near, ...), custom_call_target="tpu_custom_call" | custom-call | bytes 8388608 | tf_op jit(solution)/shard_map/grad_tokens/pallas_call | solution.py:330
  104.3 7.2 %all-to-all-done.2.came = bf16[4,144,1024]{2,1,0:T(8,128)(2,1)S(1)} async-done(((bf16[4,144,1024]{2,1,0:T(8,128)(2,1)}), bf16[4,144,1024]{2,1,0:T(8,128)(2,1)S(1)}, u32[]{:S(2)}, u32[]{:S(2)}) %all-to-all-start.2) | async-done | bytes 1179680 | tf_op jit(solution)/shard_map/values/all_to_all | solution.py:410
  111.5 0.7 copy-done.5
  112.2 0.7 values.5
  112.9 3.0 %collective-permute-start.4 = (bf16[4,144,1024]{2,1,0:T(8,128)(2,1)S(1)}, bf16[4,144,1024]{2,1,0:T(8,128)(2,1)S(1)}, u32[]{:S(2)}, u32[]{:S(2)}) collective-permute-start(bf16[4,144,1024]{2,1,0:T(8,128)(2,1)S(1)} %get-tuple-element.34.refs_3_), channel_id=1, source_target_pairs={{0,64},{64,0},{1,65},{65,1},{2,66},{66,2},{3,67},{67,3},{4,68},{68... | collective-permute-start | bytes 3538952 | tf_op jit(solution)/shard_map/refresh/ppermute | solution.py:421
  115.9 2.4 %collective-permute-done.4.refs_4_ = bf16[4,144,1024]{2,1,0:T(8,128)(2,1)S(1)} collective-permute-done((bf16[4,144,1024]{2,1,0:T(8,128)(2,1)S(1)}, bf16[4,144,1024]{2,1,0:T(8,128)(2,1)S(1)}, u32[]{:S(2)}, u32[]{:S(2)}) %collective-permute-start.4) | collective-permute-done | bytes 1179680 | tf_op jit(solution)/shard_map/refresh/ppermute | solution.py:421
  118.4 1.1 refresh.3
  (19 shorter events, 1.0 us)
Async XLA Ops:
  7.2 68.9 %all-gather.2.cloned.1.call-start = ((), (), s32[]{:S(2)}) async-start(), calls=%async_computation.3 | async-start | bytes 2359296 | tf_op jit(solution)/shard_map/weight_gather/all_gather | solution.py:395
  9.1 9.6 %collective-permute-start = (bf16[64,1024]{1,0:T(8,128)(2,1)}, bf16[64,1024]{1,0:T(8,128)(2,1)S(1)}, u32[]{:S(2)}, u32[]{:S(2)}) collective-permute-start(bf16[64,1024]{1,0:T(8,128)(2,1)} %dequant.1.refs_1_), channel_id=1, source_target_pairs={{0,4},{4,0},{1,5},{5,1},{2,6},{6,2},{3,7},{7,3},{8,12},{12,8},{9,1... | collective-permute-start | bytes 393224 | tf_op jit(solution)/shard_map/dequant/ppermute | solution.py:369
  14.0 4.8 %copy-start.3 = (bf16[64,1024]{1,0:T(8,128)(2,1)S(1)}, bf16[64,1024]{1,0:T(8,128)(2,1)}, u32[]{:S(2)}) copy-start(bf16[64,1024]{1,0:T(8,128)(2,1)} %dequant.1.refs_1_) | copy-start | bytes 393220
  18.8 0.7 copy-start.6
  20.2 7.6 %collective-permute-start.1 = (f32[64,8,128]{2,1,0:T(8,128)}, f32[64,8,128]{2,1,0:T(8,128)S(1)}, u32[]{:S(2)}, u32[]{:S(2)}) collective-permute-start(f32[64,8,128]{2,1,0:T(8,128)} %get-tuple-element.23), channel_id=1, source_target_pairs={{0,64},{64,0},{1,65},{65,1},{2,66},{66,2},{3,67},{67,3},{4,68},{68... | collective-permute-start | bytes 786440 | tf_op jit(solution)/shard_map/gradients/ppermute | solution.py:385
  27.8 1.0 copy-start.4
  28.8 47.3 %copy-start = (f32[2048,64]{0,1:T(8,128)S(1)}, f32[2048,64]{0,1:T(8,128)}, u32[]{:S(2)}) copy-start(f32[2048,64]{0,1:T(8,128)} %param.10) | copy-start | bytes 1572868
  76.2 0.8 copy-start.2
  77.0 10.0 %collective-permute-start.2 = (bf16[1024,1024]{1,0:T(8,128)(2,1)}, bf16[1024,1024]{1,0:T(8,128)(2,1)}, u32[]{:S(2)}, u32[]{:S(2)}) collective-permute-start(bf16[1024,1024]{1,0:T(8,128)(2,1)} %get-tuple-element.24.refs_2_.near), channel_id=1, source_target_pairs={{0,64},{64,0},{1,65},{65,1},{2,66},{66,2},{3,67},{67,3},{4,68},{68... | collective-permute-start | bytes 6291464 | tf_op jit(solution)/shard_map/weight_swap/ppermute | solution.py:403
  91.1 20.4 %all-to-all-start.2 = ((bf16[4,144,1024]{2,1,0:T(8,128)(2,1)}), bf16[4,144,1024]{2,1,0:T(8,128)(2,1)S(1)}, u32[]{:S(2)}, u32[]{:S(2)}) async-start(bf16[4,144,1024]{2,1,0:T(8,128)(2,1)} %values.4), calls=%async_computation.2 | async-start | bytes 2359296 | tf_op jit(solution)/shard_map/values/all_to_all | solution.py:410
  95.2 3.2 %collective-permute-start.3 = (bf16[64,1024]{1,0:T(8,128)(2,1)S(1)}, bf16[64,1024]{1,0:T(8,128)(2,1)S(1)}, u32[]{:S(2)}, u32[]{:S(2)}) collective-permute-start(bf16[64,1024]{1,0:T(8,128)(2,1)S(1)} %get-tuple-element.29.refs_2_), channel_id=1, source_target_pairs={{0,64},{64,0},{1,65},{65,1},{2,66},{66,2},{3,67},{67,3},{4,68},{68... | collective-permute-start | bytes 393224 | tf_op jit(solution)/shard_map/weight_swap/ppermute | solution.py:404
  104.3 14.1 %copy-start.1 = (f32[64,1024]{1,0:T(8,128)S(1)}, f32[64,1024]{1,0:T(8,128)}, u32[]{:S(2)}) copy-start(f32[64,1024]{1,0:T(8,128)} %refs_2_.5) | copy-start | bytes 786436
  111.5 0.7 copy-start.5
  112.9 5.5 %collective-permute-start.4 = (bf16[4,144,1024]{2,1,0:T(8,128)(2,1)S(1)}, bf16[4,144,1024]{2,1,0:T(8,128)(2,1)S(1)}, u32[]{:S(2)}, u32[]{:S(2)}) collective-permute-start(bf16[4,144,1024]{2,1,0:T(8,128)(2,1)S(1)} %get-tuple-element.34.refs_3_), channel_id=1, source_target_pairs={{0,64},{64,0},{1,65},{65,1},{2,66},{66,2},{3,67},{67,3},{4,68},{68... | collective-permute-start | bytes 3538952 | tf_op jit(solution)/shard_map/refresh/ppermute | solution.py:421
Sparse Core Ops, SparseCore 0:
  20.3 54.2 all-gather.1

commit v4 on v3

--- a/solution.py
+++ b/solution.py
@@ -75,8 +75,10 @@
         in_specs=[pl.BlockSpec(memory_space=pltpu.SMEM)] * first
         + [pl.BlockSpec(memory_space=pltpu.HBM)] * count
         + [pl.BlockSpec(memory_space=pltpu.VMEM)] * len(arrays)
-        + [pl.BlockSpec(memory_space=pl.ANY)] * len(after),
-        out_specs=jax.tree.map(lambda _: pl.BlockSpec(memory_space=pltpu.VMEM), outs),
+        + [pl.BlockSpec(memory_space=pltpu.SMEM)] * len(after),
+        out_specs=jax.tree.map(
+            lambda a: pl.BlockSpec(memory_space=pltpu.SMEM if a.shape == (1,) else pltpu.VMEM), outs
+        ),
         scratch_shapes=scratch + [pltpu.SemaphoreType.DMA((count,))] * (count > 0),
         compiler_params=pltpu.CompilerParams(vmem_limit_bytes=limit),
         cost_estimate=cost(4),
@@ -133,9 +135,9 @@
 
 
 def gradients_kernel(
-    core, tokens, cotangent, down, up, low_ref, rank_ref, send_ref, parts_ref, mark_ref
+    core, tokens, cotangent, down, up, low_ref, rank_ref, send_ref, parts_ref, mark
 ):
-    mark_ref[...] = jnp.zeros(mark_ref.shape, f32)
+    mark[0] = 0
     wide = cotangent[...]
     high, middle, low = thirds(up[...])
     back = dot(wide, low, NT) + dot(wide, middle, NT) + dot(wide, high, NT)
@@ -144,10 +146,10 @@
     own, other = halves(core[0], tokens.shape[1] // 2)
     store_tiles(send_ref, dot(back_low, tokens[:, other], TN) * INV_ROOT, 0)
     store_tiles(parts_ref, dot(back_low, tokens[:, own], TN) * INV_ROOT, 0)
-    rank = dot(tokens[...], down[...].astype(bf16), NT) * INV_ROOT
+    rank = dot(down[...].astype(bf16), tokens[...], NT) * INV_ROOT
     rank_ref[...] = rank
     high, middle, low = thirds(rank)
-    up_grad = dot(low, wide, TN) + dot(middle, wide, TN) + dot(high, wide, TN)
+    up_grad = dot(low, wide, NN) + dot(middle, wide, NN) + dot(high, wide, NN)
     store_tiles(parts_ref, adapter_scale * up_grad, 8)
 
 
@@ -203,17 +205,16 @@
     )(core, weight, down, gathered)
 
 
-def down_kernel(core, down, raw, raw_other, out, mark_ref):
-    mark_ref[...] = jnp.zeros(mark_ref.shape, f32)
+def down_kernel(core, down, raw, raw_other, out):
     own, other = halves(core[0], down.shape[1] // 2)
     out[:, own] = down[:, own] - down_learning_rate * normed(raw[...].astype(f32))
     out[:, other] = down[:, other] - down_learning_rate * normed(raw_other[...].astype(f32))
 
 
 def part_sum(rows):
-    wide = rows[0, 64:80, :].astype(f32)
+    wide = rows[0, 64:, :].astype(f32)
     for p in range(1, 4):
-        wide = wide + rows[p, 64:80, :].astype(f32)
+        wide = wide + rows[p, 64:, :].astype(f32)
     return jnp.concatenate([wide[:, 256 * i : 256 * i + 256] for i in range(4)], axis=0)
 
 
@@ -227,123 +228,36 @@
     up_ref[...] = up[:, columns] - up_learning_rate * normed(total)
 
 
-def near_values_kernel(core, tokens, weight, rank, up, out):
-    own, _ = halves(core[0], tokens.shape[1] // 2)
-    branch = lax.dot_general(
-        rank[...], up[...], NN, precision=lax.Precision.HIGHEST, preferred_element_type=f32
-    )
-    out[...] = dot(tokens[:, own], weight[...], NT) + adapter_scale * branch
-
-
-def far_values_kernel(core, tokens, weight, near, rows, out, *scratch):
-    *places, result, sems, sem = scratch
-    _, other = halves(core[0], tokens.shape[1] // 2)
-    load((tokens.at[:, other], weight, near, rows), places, sems)
-    tokens_at, weight_at, near_at, rows_at = places
-    low = (near_at[...] + dot(tokens_at[...], weight_at[...], NT)).astype(bf16)
+def values_kernel(core, tokens, near, far, rank, up, out, mark):
+    mark[0] = 0
+    own, other = halves(core[0], tokens.shape[1] // 2)
+    high, middle, low = thirds(adapter_scale * rank[...])
+    thin = jnp.concatenate([low, middle, high, middle, high, high], axis=0)
+    high, middle, low = thirds(up[...])
+    tall = jnp.concatenate([high, middle, low, high, middle, high], axis=0)
+    total = dot(near[...], tokens[:, own], NT) + dot(far[...], tokens[:, other], NT)
+    total = (total + dot(tall, thin, TN)).astype(bf16)
     for p in range(4):
-        result[p, :80, :] = rows_at[p]
-        for i in range(4):
-            result[p, 80:, 256 * i : 256 * i + 256] = low[64 * i : 64 * i + 64, 256 * p : 256 * p + 256]
-    copy = pltpu.make_async_copy(result, out, sem)
-    copy.start()
-    copy.wait()
-
-
-def far_values(core, tokens, weight, near, rows):
-    stored = pl.BlockSpec(memory_space=pltpu.HBM)
-    out = (rows.shape[0], rows.shape[1] + 64, rows.shape[2])
-    return pl.pallas_call(
-        far_values_kernel,
-        out_shape=shape(*out, dtype=bf16),
-        in_specs=[pl.BlockSpec(memory_space=pltpu.SMEM)] + [stored] * 4,
-        out_specs=stored,
-        scratch_shapes=[
-            pltpu.VMEM((tokens.shape[0], tokens.shape[1] // 2), bf16),
-            pltpu.VMEM(weight.shape, bf16),
-            pltpu.VMEM(near.shape, f32),
-            pltpu.VMEM(rows.shape, bf16),
-            pltpu.VMEM(out, bf16),
-            pltpu.SemaphoreType.DMA((4,)),
-            pltpu.SemaphoreType.DMA,
-        ],
-        compiler_params=pltpu.CompilerParams(vmem_limit_bytes=WHOLE),
-        cost_estimate=cost(8),
-    )(core, tokens, weight, near, rows)
-
-
-def sum_values_kernel(came, mark_1, mark_2, out, same):
-    del mark_1, mark_2, same
-    for i in range(4):
-        total = came[0, 80:, 256 * i : 256 * i + 256].astype(f32)
-        for p in range(1, 4):
-            total = total + came[p, 80:, 256 * i : 256 * i + 256].astype(f32)
-        out[64 * i : 64 * i + 64, :] = total.astype(bf16)
-
-
-def sum_values(came, mark_1, mark_2):
-    here, anywhere = pl.BlockSpec(memory_space=pltpu.VMEM), pl.BlockSpec(memory_space=pl.ANY)
-    return pl.pallas_call(
-        sum_values_kernel,
-        out_shape=(shape(256, 256, dtype=bf16), shape(*came.shape, dtype=bf16)),
-        in_specs=[here, anywhere, anywhere],
-        out_specs=(here, here),
-        input_output_aliases={0: 1},
-        compiler_params=pltpu.CompilerParams(vmem_limit_bytes=LIMIT),
-        cost_estimate=cost(4),
-    )(came, mark_1, mark_2)
-
-
-def token_gradients_kernel(core, cotangent, low, down, near, far, out, mark_ref, *scratch):
-    mark_ref[...] = jnp.zeros(mark_ref.shape, f32)
-    wide, thin, master, matrices, result, sems, out_sems = scratch
-    width = matrices.shape[2]
-    sources = (cotangent, low, down, near, far)
-    places = (wide, thin, master, matrices.at[0], matrices.at[1])
-    loads = [pltpu.make_async_copy(a, b, sems.at[i]) for i, (a, b) in enumerate(zip(sources, places))]
-    for copy in loads:
-        copy.start()
-    for copy in loads[:3]:
-        copy.wait()
-    stores = []
-    for h, place in enumerate(halves(core[0], width)):
-        loads[3 + h].wait()
-        for q in range(2):
-            step = width // 2
-            columns = pl.ds(pl.multiple_of(place.start + step * q, step), step)
-            part = pl.ds(step * q, step)
-            beside = dot(thin[...], master[:, columns].astype(bf16), NN) * INV_ROOT
-            result[h, :, part] = (dot(wide[...], matrices[h, :, part], NN) + beside).astype(bf16)
-            stores.append(
-                pltpu.make_async_copy(
-                    result.at[h, :, part], out.at[:, columns], out_sems.at[2 * h + q]
-                )
-            )
-            stores[-1].start()
-    for copy in stores:
-        copy.wait()
-
-
-def token_gradients(core, cotangent, low, down, near, far):
-    rows, columns = cotangent.shape[0], down.shape[1]
-    stored = pl.BlockSpec(memory_space=pltpu.HBM)
-    return pl.pallas_call(
-        token_gradients_kernel,
-        out_shape=(shape(rows, columns, dtype=bf16), shape(8, 128)),
-        in_specs=[pl.BlockSpec(memory_space=pltpu.SMEM)] + [stored] * 5,
-        out_specs=(stored, pl.BlockSpec(memory_space=pltpu.VMEM)),
-        scratch_shapes=[
-            pltpu.VMEM(cotangent.shape, bf16),
-            pltpu.VMEM(low.shape, bf16),
-            pltpu.VMEM(down.shape, f32),
-            pltpu.VMEM((2, *near.shape), bf16),
-            pltpu.VMEM((2, rows, columns // 2), bf16),
-            pltpu.SemaphoreType.DMA((5,)),
-            pltpu.SemaphoreType.DMA((4,)),
-        ],
-        compiler_params=pltpu.CompilerParams(vmem_limit_bytes=WHOLE),
-        cost_estimate=cost(8),
-    )(core, cotangent, low, down, near, far)
+        out[p] = total[256 * p : 256 * p + 256]
+
+
+def sum_values_kernel(came, out):
+    total = came[0].astype(f32)
+    for p in range(1, 4):
+        total = total + came[p].astype(f32)
+    out[...] = total.T.astype(bf16)
+
+
+def copy_kernel(rows, out):
+    out[...] = rows[...]
+
+
+def token_gradients_kernel(core, cotangent, low, down, near, far, out, mark):
+    mark[0] = 0
+    width = near.shape[1]
+    for place, weight in zip(halves(core[0], width), (near, far)):
+        beside = dot(low[...], down[:, place].astype(bf16), NN) * INV_ROOT
+        out[:, place] = (dot(cotangent[...], weight[...], NN) + beside).astype(bf16)
 
 
 def body(tokens, cotangent, codes, scales, adapter_down, adapter_up):
@@ -354,7 +268,7 @@
     swap = [(0, 1), (1, 0)]
     half = codes.shape[0] // 2
 
-    mark = shape(8, 128)
+    mark = shape(1, dtype=jnp.int32)
     z_low = lax.axis_index("zl").astype(jnp.int32).reshape(1)
 
     with jax.named_scope("dequant"):
@@ -372,7 +286,7 @@
             gradients_kernel,
             (
                 shape(256, 64, dtype=bf16),
-                shape(256, 64),
+                shape(64, 256),
                 shape(64, 8, 128),
                 shape(64, 16, 128),
                 mark,
@@ -398,33 +312,42 @@
         parts = lax.all_to_all(parts, PLANE, 0, 0, tiled=True)
         total = call(total_kernel, shape(64, 16, 128, dtype=bf16), (), (), (parts,))
         gathered = lax.all_to_all(total, PLANE, 0, 0, tiled=True)
-    with jax.named_scope("weight_swap"):
+    with jax.named_scope("refresh"):
         rows, raw, near = scorer_rows(core, weight, down, gathered)
+        rows = lax.all_to_all(rows, "x", 0, 0, tiled=True)
+    with jax.named_scope("values"):
         far = lax.ppermute(near, "c", swap)
+        sent, whole = call(
+            values_kernel,
+            (shape(4, 256, 256, dtype=bf16), mark),
+            (core,),
+            (),
+            (tokens, near, far, rank, adapter_up),
+        )
+        came = lax.all_to_all(sent, "x", 0, 0, tiled=True)
+        values = call(sum_values_kernel, shape(256, 256, dtype=bf16), (), (), (came,))
+    with jax.named_scope("grad_tokens"):
+        grad_tokens, turned = call(
+            token_gradients_kernel,
+            (shape(256, 2048, dtype=bf16), mark),
+            (core,),
+            (),
+            (cotangent, back_low, down, near, far),
+            after=(whole,),
+        )
+    with jax.named_scope("refresh"):
         raw_other = lax.ppermute(raw, "c", swap)
-    with jax.named_scope("values"):
-        near_part = call(
-            near_values_kernel, shape(256, 1024), (core,), (tokens, near, rank, adapter_up), (), WHOLE
-        )
-        sent = far_values(core, tokens, far, near_part, rows)
-        came = lax.all_to_all(sent, "x", 0, 0, tiled=True)
-    with jax.named_scope("refresh"):
-        refreshed_down, refreshed = call(
-            down_kernel, (shape(64, 2048), mark), (core,), (), (down, raw, raw_other)
-        )
-        refreshed_down = refreshed_down.T
-    with jax.named_scope("grad_tokens"):
-        grad_tokens, turned = token_gradients(core, cotangent, back_low, down, near, far)
-    with jax.named_scope("values"):
-        values, came = sum_values(came, turned, refreshed)
-    with jax.named_scope("refresh"):
-        came_other = lax.ppermute(came, "c", swap)
+        refreshed_down = call(
+            down_kernel, shape(64, 2048), (core,), (), (down, raw, raw_other), after=(whole,)
+        ).T
+        rows = call(copy_kernel, shape(*rows.shape, dtype=bf16), (), (), (rows,), after=(turned,))
+        rows_other = lax.ppermute(rows, "c", swap)
         scorer_a, refreshed_up = call(
             finish_kernel,
             (shape(64, 8192, dtype=bf16), shape(64, 256)),
             (core, place),
             (),
-            (adapter_up, came, came_other),
+            (adapter_up, rows, rows_other),
         )
         scorer_a = scorer_a.T
     return (values, grad_tokens, refreshed_down, scorer_a, refreshed_up)

time: 127 us -> 124 us (0.976)
  waiting for transfers between devices: 12.1 us -> 6.92 us
  starting transfers between devices: 25.9 us -> 30.4 us
  Pallas kernels: 23.7 us -> 20.3 us
  local copies, waits for them, and re-layouts: 3.26 us -> 5.42 us
    pallas_call x3 -> x0, Pallas kernels: 9.73 us -> none  [the longest x1 4.97 us: token_gradients(): pl.pallas_call(token_gradients_kernel, out_shape=(shape(rows, columns, dt...]
    pallas_call x8 -> x11, Pallas kernels: 13.9 us -> 20.2 us  [call(): pl.pallas_call(loaded, out_shape=outs, in_specs=[pl.BlockSpec(memory_spac...]
    all_to_all x0 -> x1, starting transfers between devices: none -> 4.34 us  [body(): rows = lax.all_to_all(rows, 'x', 0, 0, tiled=True)]
    all_to_all x1, waiting for transfers between devices: 7.24 us -> 4.51 us  [body(): came = lax.all_to_all(sent, 'x', 0, 0, tiled=True)]
    ppermute x1, waiting for transfers between devices: 2.45 us -> 0.01 us  [body(): rows_other = lax.ppermute(rows, 'c', swap)]
    unnamed x14 -> x24, local copies, waits for them, and re-layouts: 3.26 us -> 5.42 us
  transfers between devices with their start and end apart: 7 -> 8, of which waited for: 4 -> 3; matrix products, arithmetic and copies ran while one was open for 0% -> 0% of each run, Pallas kernels for 12% -> 12%
where the time goes in v4:
time: 124 us; the launch traced here: 123 us
  blocking collectives  46.1 us (37%)
  starting transfers between devices  30.4 us (25%)
  Pallas kernels  20.3 us (16%)
  between operations  14.2 us (11%)
  waiting for transfers between devices  6.92 us (6%)
  local copies, waits for them, and re-layouts  5.42 us (4%)
    all_to_all x1, blocking collectives, body(): parts = lax.all_to_all(parts, PLANE, 0, 0, tiled=True)  27.2 us
    pallas_call x11, Pallas kernels, call(): pl.pallas_call(loaded, out_shape=outs, in_specs=[pl.BlockSpec(memory_spac...  20.2 us
    all_to_all x1, blocking collectives, body(): gathered = lax.all_to_all(total, PLANE, 0, 0, tiled=True)  18.9 us
    ppermute x1, starting transfers between devices, body(): arrived = lax.ppermute(send, 'c', swap)  6.22 us
    ppermute x1, starting transfers between devices, body(): far = lax.ppermute(near, 'c', swap)  5.89 us
    unnamed x24, local copies, waits for them, and re-layouts  5.42 us
    ppermute x1, starting transfers between devices, body(): theirs = lax.ppermute(mine, 'zl', swap)  4.96 us
    all_to_all x1, waiting for transfers between devices, body(): came = lax.all_to_all(sent, 'x', 0, 0, tiled=True)  4.51 us
  transfers between devices with their start and end apart: 8, of which 3 were waited for; matrix products, arithmetic and copies ran while one was open for 0% of the time, Pallas kernels for 12%

profile of v4, /device:TPU:1, one launch (start us, length us, event | category | flops | bytes accessed | tf_op | source)
XLA Modules:
  0.0 123.3 jit_solution(15116002862616756949)
XLA Ops:
  7.2 1.9 %dequant.1.refs_1_ = bf16[64,1024]{1,0:T(8,128)(2,1)} custom-call(s32[1]{0:T(128)} %bitcast.refs_0_.core, bf16[64,2048]{1,0:T(8,128)(2,1)} %bitcast.12, bf16[16,64]{1,0:T(8,128)(2,1)} %refs_2_.3), custom_call_target="tpu_custom_call" | custom-call | bytes 4194304 | tf_op jit(solution)/shard_map/dequant/pallas_call | solution.py:72
  9.1 5.0 %collective-permute-start = (bf16[64,1024]{1,0:T(8,128)(2,1)}, bf16[64,1024]{1,0:T(8,128)(2,1)S(1)}, u32[]{:S(2)}, u32[]{:S(2)}) collective-permute-start(bf16[64,1024]{1,0:T(8,128)(2,1)} %dequant.1.refs_1_), channel_id=1, source_target_pairs={{0,4},{4,0},{1,5},{5,1},{2,6},{6,2},{3,7},{7,3},{8,12},{12,8},{9,1... | collective-permute-start | bytes 393224 | tf_op jit(solution)/shard_map/dequant/ppermute | solution.py:283
  14.1 4.7 %gradients.1 = (bf16[256,64]{1,0:T(8,128)(2,1)}, f32[64,256]{1,0:T(8,128)}, f32[64,8,128]{2,1,0:T(8,128)}, f32[64,16,128]{2,1,0:T(8,128)}, s32[1]{0:T(128)}) custom-call(s32[1]{0:T(128)} %bitcast.refs_0_.core, bf16[256,2048]{1,0:T(8,128)(2,1)} %refs_1_.4, bf16[256,1024]{1,0:T(8,128)(2,1)} %refs_1_.5, f32[64,2048]{1,0:T(8,128)} %bitcast.7, f32[64,1024]{1,0:T(8,128)} %refs_2_.5), custom_call_target="tpu_custom_call" | custom-call | bytes 4194304 | tf_op jit(solution)/shard_map/gradients/pallas_call | solution.py:72
  18.9 1.3 %weight_gather.1 = bf16[128,1024]{1,0:T(8,128)(2,1)} custom-call(s32[1]{0:T(128)} %bitcast.1.refs_0_, bf16[64,1024]{1,0:T(8,128)(2,1)S(1)} %copy-done.7, bf16[64,1024]{1,0:T(8,128)(2,1)S(1)} %collective-permute-done.refs_2_, s32[1]{0:T(128)} %get-tuple-element.19.refs_3_), custom_call_target="tpu_custom_call" | custom-call | bytes 4194304 | tf_op jit(solution)/shard_map/weight_gather/pallas_call | solution.py:72
  20.2 6.2 %collective-permute-start.1 = (f32[64,8,128]{2,1,0:T(8,128)}, f32[64,8,128]{2,1,0:T(8,128)S(1)}, u32[]{:S(2)}, u32[]{:S(2)}) collective-permute-start(f32[64,8,128]{2,1,0:T(8,128)} %get-tuple-element.21), channel_id=1, source_target_pairs={{0,64},{64,0},{1,65},{65,1},{2,66},{66,2},{3,67},{67,3},{4,68},{68... | collective-permute-start | bytes 786440 | tf_op jit(solution)/shard_map/gradients/ppermute | solution.py:299
  26.4 1.4 %collective-permute-done.1.refs_1_ = f32[64,8,128]{2,1,0:T(8,128)S(1)} collective-permute-done((f32[64,8,128]{2,1,0:T(8,128)}, f32[64,8,128]{2,1,0:T(8,128)S(1)}, u32[]{:S(2)}, u32[]{:S(2)}) %collective-permute-start.1) | collective-permute-done | bytes 262176 | tf_op jit(solution)/shard_map/gradients/ppermute | solution.py:299
  27.8 1.0 copy-done.6
  28.9 27.2 %all_to_all.20.refs_0_ = bf16[64,16,128]{2,1,0:T(8,128)(2,1)S(1)} all-to-all(bf16[64,16,128]{2,1,0:T(8,128)(2,1)S(1)} %plane_sum.2), channel_id=1, replica_groups=mesh['zh'=4,'c'=2,'y'=8,'zl'=2,'x'=4] {'zh','y','zl'}, dimensions={0} | all-to-all | bytes 524288 | tf_op jit(solution)/shard_map/plane_sum/all_to_all | solution.py:312
  56.2 18.9 %all_to_all.21.gathered = bf16[64,16,128]{2,1,0:T(8,128)(2,1)S(1)} all-to-all(bf16[64,16,128]{2,1,0:T(8,128)(2,1)S(1)} %plane_sum.3), channel_id=1, replica_groups=mesh['zh'=4,'c'=2,'y'=8,'zl'=2,'x'=4] {'zh','y','zl'}, dimensions={0} | all-to-all | bytes 524288 | tf_op jit(solution)/shard_map/plane_sum/all_to_all | solution.py:314
  75.2 0.8 copy-done.4
  76.7 5.9 %collective-permute-start.2 = (bf16[1024,1024]{1,0:T(8,128)(2,1)}, bf16[1024,1024]{1,0:T(8,128)(2,1)S(1)}, u32[]{:S(2)}, u32[]{:S(2)}) collective-permute-start(bf16[1024,1024]{1,0:T(8,128)(2,1)} %get-tuple-element.22.refs_2_.refs_4_), channel_id=1, source_target_pairs={{0,64},{64,0},{1,65},{65,1},{2,66},{66,2},{3,67},{67,3},{4,68},{68... | collective-permute-start | bytes 6291464 | tf_op jit(solution)/shard_map/values/ppermute | solution.py:319
  82.6 4.3 %all-to-all-start.3 = ((bf16[4,80,1024]{2,1,0:T(8,128)(2,1)}), bf16[4,80,1024]{2,1,0:T(8,128)(2,1)S(1)}, u32[]{:S(2)}, u32[]{:S(2)}) async-start(bf16[4,80,1024]{2,1,0:T(8,128)(2,1)} %copy-done.4), calls=%async_computation.3 | async-start | bytes 1310720 | tf_op jit(solution)/shard_map/refresh/all_to_all | solution.py:317
  87.0 1.2 copy-done.1
  88.2 0.8 copy-done.11
  89.0 3.2 %values.2 = (bf16[4,256,256]{2,1,0:T(8,128)(2,1)S(1)}, s32[1]{0:T(128)}) custom-call(s32[1]{0:T(128)} %bitcast.refs_0_.core, bf16[256,2048]{1,0:T(8,128)(2,1)S(1)} %copy-done.1, bf16[1024,1024]{1,0:T(8,128)(2,1)} %get-tuple-element.22.refs_2_.refs_4_, bf16[1024,1024]{1,0:T(8,128)(2,1)S(1)} %collective-permute-done.2.refs_3_.refs_5_, ...), custom_call_target="tpu_custom_call" | custom-call | bytes 4194304 | tf_op jit(solution)/shard_map/values/pallas_call | solution.py:72
  92.3 0.8 copy-done.5
  93.1 4.8 %grad_tokens.1 = (bf16[256,2048]{1,0:T(8,128)(2,1)}, s32[1]{0:T(128)}) custom-call(s32[1]{0:T(128)} %bitcast.refs_0_.core, bf16[256,1024]{1,0:T(8,128)(2,1)S(1)} %copy-done.3, bf16[256,64]{1,0:T(8,128)(2,1)S(1)} %copy-done.10, f32[64,2048]{1,0:T(8,128)S(1)} %bitcast.9, bf16[1024,1024]{1,0:T(8,128)(2,1)} %get-tuple-element.22.refs_2_.refs_4_, ...), custom_call_target="tpu_custom_call" | custom-call | bytes 4194304 | tf_op jit(solution)/shard_map/grad_tokens/pallas_call | solution.py:72
  98.6 2.8 %collective-permute-start.4 = (bf16[4,80,1024]{2,1,0:T(8,128)(2,1)S(1)}, bf16[4,80,1024]{2,1,0:T(8,128)(2,1)S(1)}, u32[]{:S(2)}, u32[]{:S(2)}) collective-permute-start(bf16[4,80,1024]{2,1,0:T(8,128)(2,1)S(1)} %refresh.6.refs_3_), channel_id=1, source_target_pairs={{0,64},{64,0},{1,65},{65,1},{2,66},{66,2},{3,67},{67,3},{4,68},{68... | collective-permute-start | bytes 1966088 | tf_op jit(solution)/shard_map/refresh/ppermute | solution.py:344
  101.4 3.9 %all-to-all-start.2 = ((bf16[4,256,256]{2,1,0:T(8,128)(2,1)}), bf16[4,256,256]{2,1,0:T(8,128)(2,1)S(1)}, u32[]{:S(2)}, u32[]{:S(2)}) async-start(bf16[4,256,256]{2,1,0:T(8,128)(2,1)} %copy-done.5), calls=%async_computation.2 | async-start | bytes 1048576 | tf_op jit(solution)/shard_map/values/all_to_all | solution.py:327
  105.3 2.2 %collective-permute-start.3 = (bf16[64,1024]{1,0:T(8,128)(2,1)S(1)}, bf16[64,1024]{1,0:T(8,128)(2,1)S(1)}, u32[]{:S(2)}, u32[]{:S(2)}) collective-permute-start(bf16[64,1024]{1,0:T(8,128)(2,1)S(1)} %copy-done.9), channel_id=1, source_target_pairs={{0,64},{64,0},{1,65},{65,1},{2,66},{66,2},{3,67},{67,3},{4,68},{68... | collective-permute-start | bytes 393224 | tf_op jit(solution)/shard_map/refresh/ppermute | solution.py:339
  107.5 1.0 collective-permute-done.3.refs_3_
  108.5 1.6 %refresh.5 = f32[64,2048]{1,0:T(8,128)} custom-call(s32[1]{0:T(128)} %bitcast.refs_0_.core, f32[64,2048]{1,0:T(8,128)S(1)} %bitcast.10, bf16[64,1024]{1,0:T(8,128)(2,1)S(1)} %copy-done.9, bf16[64,1024]{1,0:T(8,128)(2,1)S(1)} %collective-permute-done.3.refs_3_, s32[1]{0:T(128)} %get-tuple-element.26.refs_6_.refs_4_), custom_call_target="tpu_custom_call" | custom-call | bytes 4194304 | tf_op jit(solution)/shard_map/refresh/pallas_call | solution.py:72
  110.1 4.5 %all-to-all-done.2.refs_0_ = bf16[4,256,256]{2,1,0:T(8,128)(2,1)S(1)} async-done(((bf16[4,256,256]{2,1,0:T(8,128)(2,1)}), bf16[4,256,256]{2,1,0:T(8,128)(2,1)S(1)}, u32[]{:S(2)}, u32[]{:S(2)}) %all-to-all-start.2) | async-done | bytes 524320 | tf_op jit(solution)/shard_map/values/all_to_all | solution.py:327
  115.4 1.1 refresh.7
  (31 shorter events, 2.5 us)
Async XLA Ops:
  7.2 68.0 %all-gather.2.cloned.1.call-start = ((), (), s32[]{:S(2)}) async-start(), calls=%async_computation.4 | async-start | bytes 2359296 | tf_op jit(solution)/shard_map/weight_gather/all_gather | solution.py:309
  9.1 9.7 %copy-start.7 = (bf16[64,1024]{1,0:T(8,128)(2,1)S(1)}, bf16[64,1024]{1,0:T(8,128)(2,1)}, u32[]{:S(2)}) copy-start(bf16[64,1024]{1,0:T(8,128)(2,1)} %dequant.1.refs_1_) | copy-start | bytes 393220
  9.1 9.7 %collective-permute-start = (bf16[64,1024]{1,0:T(8,128)(2,1)}, bf16[64,1024]{1,0:T(8,128)(2,1)S(1)}, u32[]{:S(2)}, u32[]{:S(2)}) collective-permute-start(bf16[64,1024]{1,0:T(8,128)(2,1)} %dequant.1.refs_1_), channel_id=1, source_target_pairs={{0,4},{4,0},{1,5},{5,1},{2,6},{6,2},{3,7},{7,3},{8,12},{12,8},{9,1... | collective-permute-start | bytes 393224 | tf_op jit(solution)/shard_map/dequant/ppermute | solution.py:283
  18.8 56.3 %copy-start = (f32[2048,64]{0,1:T(8,128)S(1)}, f32[2048,64]{0,1:T(8,128)}, u32[]{:S(2)}) copy-start(f32[2048,64]{0,1:T(8,128)} %param.10) | copy-start | bytes 1572868
  20.2 7.6 %collective-permute-start.1 = (f32[64,8,128]{2,1,0:T(8,128)}, f32[64,8,128]{2,1,0:T(8,128)S(1)}, u32[]{:S(2)}, u32[]{:S(2)}) collective-permute-start(f32[64,8,128]{2,1,0:T(8,128)} %get-tuple-element.21), channel_id=1, source_target_pairs={{0,64},{64,0},{1,65},{65,1},{2,66},{66,2},{3,67},{67,3},{4,68},{68... | collective-permute-start | bytes 786440 | tf_op jit(solution)/shard_map/gradients/ppermute | solution.py:299
  27.8 1.0 copy-start.6
  75.1 11.8 %copy-start.2 = (f32[64,1024]{1,0:T(8,128)S(1)}, f32[64,1024]{1,0:T(8,128)}, u32[]{:S(2)}) copy-start(f32[64,1024]{1,0:T(8,128)} %refs_2_.5) | copy-start | bytes 786436
  75.2 0.8 copy-start.4
  76.1 0.7 copy-start.8
  76.7 10.2 %collective-permute-start.2 = (bf16[1024,1024]{1,0:T(8,128)(2,1)}, bf16[1024,1024]{1,0:T(8,128)(2,1)S(1)}, u32[]{:S(2)}, u32[]{:S(2)}) collective-permute-start(bf16[1024,1024]{1,0:T(8,128)(2,1)} %get-tuple-element.22.refs_2_.refs_4_), channel_id=1, source_target_pairs={{0,64},{64,0},{1,65},{65,1},{2,66},{66,2},{3,67},{67,3},{4,68},{68... | collective-permute-start | bytes 6291464 | tf_op jit(solution)/shard_map/values/ppermute | solution.py:319
  82.6 15.2 %all-to-all-start.3 = ((bf16[4,80,1024]{2,1,0:T(8,128)(2,1)}), bf16[4,80,1024]{2,1,0:T(8,128)(2,1)S(1)}, u32[]{:S(2)}, u32[]{:S(2)}) async-start(bf16[4,80,1024]{2,1,0:T(8,128)(2,1)} %copy-done.4), calls=%async_computation.3 | async-start | bytes 1310720 | tf_op jit(solution)/shard_map/refresh/all_to_all | solution.py:317
  87.0 1.2 copy-start.1
  88.2 0.8 copy-start.11
  89.0 4.0 %copy-start.3 = (bf16[256,1024]{1,0:T(8,128)(2,1)S(1)}, bf16[256,1024]{1,0:T(8,128)(2,1)}, u32[]{:S(2)}) copy-start(bf16[256,1024]{1,0:T(8,128)(2,1)} %refs_1_.5) | copy-start | bytes 1572868
  89.0 4.0 %copy-start.10 = (bf16[256,64]{1,0:T(8,128)(2,1)S(1)}, bf16[256,64]{1,0:T(8,128)(2,1)}, u32[]{:S(2)}) copy-start(bf16[256,64]{1,0:T(8,128)(2,1)} %get-tuple-element.25.refs_2_) | copy-start | bytes 98308
  92.2 0.8 copy-start.5
  97.8 7.5 %copy-start.9 = (bf16[64,1024]{1,0:T(8,128)(2,1)S(1)}, bf16[64,1024]{1,0:T(8,128)(2,1)}, u32[]{:S(2)}) copy-start(bf16[64,1024]{1,0:T(8,128)(2,1)} %copy-done.8) | copy-start | bytes 393220
  98.6 16.8 %collective-permute-start.4 = (bf16[4,80,1024]{2,1,0:T(8,128)(2,1)S(1)}, bf16[4,80,1024]{2,1,0:T(8,128)(2,1)S(1)}, u32[]{:S(2)}, u32[]{:S(2)}) collective-permute-start(bf16[4,80,1024]{2,1,0:T(8,128)(2,1)S(1)} %refresh.6.refs_3_), channel_id=1, source_target_pairs={{0,64},{64,0},{1,65},{65,1},{2,66},{66,2},{3,67},{67,3},{4,68},{68... | collective-permute-start | bytes 1966088 | tf_op jit(solution)/shard_map/refresh/ppermute | solution.py:344
  101.4 13.2 %all-to-all-start.2 = ((bf16[4,256,256]{2,1,0:T(8,128)(2,1)}), bf16[4,256,256]{2,1,0:T(8,128)(2,1)S(1)}, u32[]{:S(2)}, u32[]{:S(2)}) async-start(bf16[4,256,256]{2,1,0:T(8,128)(2,1)} %copy-done.5), calls=%async_computation.2 | async-start | bytes 1048576 | tf_op jit(solution)/shard_map/values/all_to_all | solution.py:327
  105.3 3.2 %collective-permute-start.3 = (bf16[64,1024]{1,0:T(8,128)(2,1)S(1)}, bf16[64,1024]{1,0:T(8,128)(2,1)S(1)}, u32[]{:S(2)}, u32[]{:S(2)}) collective-permute-start(bf16[64,1024]{1,0:T(8,128)(2,1)S(1)} %copy-done.9), channel_id=1, source_target_pairs={{0,64},{64,0},{1,65},{65,1},{2,66},{66,2},{3,67},{67,3},{4,68},{68... | collective-permute-start | bytes 393224 | tf_op jit(solution)/shard_map/refresh/ppermute | solution.py:339
Sparse Core Ops, SparseCore 0:
  20.3 54.1 all-gather.1

commit v5 on v4

--- a/solution.py
+++ b/solution.py
@@ -134,9 +134,7 @@
     out[count:] = jnp.where(first, theirs[...], mine[...])
 
 
-def gradients_kernel(
-    core, tokens, cotangent, down, up, low_ref, rank_ref, send_ref, parts_ref, mark
-):
+def down_gradient_kernel(core, tokens, cotangent, up, low_ref, send_ref, keep_ref, mark):
     mark[0] = 0
     wide = cotangent[...]
     high, middle, low = thirds(up[...])
@@ -145,17 +143,20 @@
     low_ref[...] = back_low
     own, other = halves(core[0], tokens.shape[1] // 2)
     store_tiles(send_ref, dot(back_low, tokens[:, other], TN) * INV_ROOT, 0)
-    store_tiles(parts_ref, dot(back_low, tokens[:, own], TN) * INV_ROOT, 0)
+    store_tiles(keep_ref, dot(back_low, tokens[:, own], TN) * INV_ROOT, 0)
+
+
+def up_gradient_kernel(tokens, cotangent, down, tiles_ref):
+    wide = cotangent[...]
     rank = dot(down[...].astype(bf16), tokens[...], NT) * INV_ROOT
-    rank_ref[...] = rank
     high, middle, low = thirds(rank)
     up_grad = dot(low, wide, NN) + dot(middle, wide, NN) + dot(high, wide, NN)
-    store_tiles(parts_ref, adapter_scale * up_grad, 8)
-
-
-def parts_kernel(parts, arrived, out):
+    store_tiles(tiles_ref, adapter_scale * up_grad, 0)
+
+
+def parts_kernel(keep, tiles, arrived, out):
     for i in range(out.shape[0]):
-        both = jnp.concatenate([parts[i, :8] + arrived[i], parts[i, 8:]], axis=0)
+        both = jnp.concatenate([keep[i] + arrived[i], tiles[i]], axis=0)
         out[i] = both.astype(bf16)
 
 
@@ -228,10 +229,11 @@
     up_ref[...] = up[:, columns] - up_learning_rate * normed(total)
 
 
-def values_kernel(core, tokens, near, far, rank, up, out, mark):
+def values_kernel(core, tokens, near, far, down, up, out, mark):
     mark[0] = 0
     own, other = halves(core[0], tokens.shape[1] // 2)
-    high, middle, low = thirds(adapter_scale * rank[...])
+    rank = dot(down[...].astype(bf16), tokens[...], NT) * INV_ROOT
+    high, middle, low = thirds(adapter_scale * rank)
     thin = jnp.concatenate([low, middle, high, middle, high, high], axis=0)
     high, middle, low = thirds(up[...])
     tall = jnp.concatenate([high, middle, low, high, middle, high], axis=0)
@@ -282,21 +284,18 @@
         )
         theirs = lax.ppermute(mine, "zl", swap)
     with jax.named_scope("gradients"):
-        back_low, rank, send, parts, begun = call(
-            gradients_kernel,
-            (
-                shape(256, 64, dtype=bf16),
-                shape(64, 256),
-                shape(64, 8, 128),
-                shape(64, 16, 128),
-                mark,
-            ),
+        back_low, send, keep, begun = call(
+            down_gradient_kernel,
+            (shape(256, 64, dtype=bf16), shape(64, 8, 128), shape(64, 8, 128), mark),
             (core,),
-            (tokens, cotangent, down, adapter_up),
+            (tokens, cotangent, adapter_up),
             (),
             WHOLE,
         )
         arrived = lax.ppermute(send, "c", swap)
+        up_tiles = call(
+            up_gradient_kernel, shape(64, 8, 128), (), (tokens, cotangent, down), (), WHOLE
+        )
     with jax.named_scope("weight_gather"):
         pair = call(
             pair_kernel,
@@ -308,7 +307,9 @@
         )
         weight = lax.all_gather(pair, "y", axis=0, tiled=True)
     with jax.named_scope("plane_sum"):
-        parts = call(parts_kernel, shape(64, 16, 128, dtype=bf16), (), (), (parts, arrived))
+        parts = call(
+            parts_kernel, shape(64, 16, 128, dtype=bf16), (), (), (keep, up_tiles, arrived)
+        )
         parts = lax.all_to_all(parts, PLANE, 0, 0, tiled=True)
         total = call(total_kernel, shape(64, 16, 128, dtype=bf16), (), (), (parts,))
         gathered = lax.all_to_all(total, PLANE, 0, 0, tiled=True)
@@ -322,7 +323,7 @@
             (shape(4, 256, 256, dtype=bf16), mark),
             (core,),
             (),
-            (tokens, near, far, rank, adapter_up),
+            (tokens, near, far, down, adapter_up),
         )
         came = lax.all_to_all(sent, "x", 0, 0, tiled=True)
         values = call(sum_values_kernel, shape(256, 256, dtype=bf16), (), (), (came,))

time: 124 us -> 124 us (level)
  Pallas kernels: 20.3 us -> 25.5 us
  local copies, waits for them, and re-layouts: 5.42 us -> 1.87 us
    pallas_call x11 -> x12, Pallas kernels: 20.2 us -> 24.6 us  [call(): pl.pallas_call(loaded, out_shape=outs, in_specs=[pl.BlockSpec(memory_spac...]
    unnamed x24 -> x16, local copies, waits for them, and re-layouts: 5.42 us -> 1.87 us
    all_to_all x1, blocking collectives: 27.2 us -> 25.7 us  [body(): parts = lax.all_to_all(parts, PLANE, 0, 0, tiled=True)]
    ppermute x1, starting transfers between devices: 6.22 us -> 7.7 us  [body(): arrived = lax.ppermute(send, 'c', swap)]
    ppermute x1, starting transfers between devices: 5.89 us -> 4.53 us  [body(): far = lax.ppermute(near, 'c', swap)]
    ppermute x1, waiting for transfers between devices: 1.35 us -> 0.01 us  [body(): arrived = lax.ppermute(send, 'c', swap)]
  transfers between devices with their start and end apart: 8 -> 8, of which waited for: 3 -> 3; matrix products, arithmetic and copies ran while one was open for 0% -> 0% of each run, Pallas kernels for 12% -> 16%
where the time goes in v5:
time: 124 us; the launch traced here: 123 us
  blocking collectives  45.7 us (37%)
  starting transfers between devices  29.7 us (24%)
  Pallas kernels  25.5 us (21%)
  between operations  14.2 us (11%)
  waiting for transfers between devices  6.26 us (5%)
  local copies, waits for them, and re-layouts  1.87 us (2%)
    all_to_all x1, blocking collectives, body(): parts = lax.all_to_all(parts, PLANE, 0, 0, tiled=True)  25.7 us
    pallas_call x12, Pallas kernels, call(): pl.pallas_call(loaded, out_shape=outs, in_specs=[pl.BlockSpec(memory_spac...  24.6 us
    all_to_all x1, blocking collectives, body(): gathered = lax.all_to_all(total, PLANE, 0, 0, tiled=True)  20 us
    ppermute x1, starting transfers between devices, body(): arrived = lax.ppermute(send, 'c', swap)  7.7 us
    ppermute x1, starting transfers between devices, body(): theirs = lax.ppermute(mine, 'zl', swap)  4.83 us
    all_to_all x1, waiting for transfers between devices, body(): came = lax.all_to_all(sent, 'x', 0, 0, tiled=True)  4.64 us
    ppermute x1, starting transfers between devices, body(): far = lax.ppermute(near, 'c', swap)  4.53 us
    all_to_all x1, starting transfers between devices, body(): rows = lax.all_to_all(rows, 'x', 0, 0, tiled=True)  4.08 us
  transfers between devices with their start and end apart: 8, of which 3 were waited for; matrix products, arithmetic and copies ran while one was open for 0% of the time, Pallas kernels for 16%

profile of v5, /device:TPU:1, one launch (start us, length us, event | category | flops | bytes accessed | tf_op | source)
XLA Modules:
  0.0 123.2 jit_solution(2340325775594400041)
XLA Ops:
  7.2 1.9 %dequant.1.refs_1_ = bf16[64,1024]{1,0:T(8,128)(2,1)} custom-call(s32[1]{0:T(128)} %bitcast.refs_0_.core, bf16[64,2048]{1,0:T(8,128)(2,1)} %bitcast.13, bf16[16,64]{1,0:T(8,128)(2,1)} %refs_2_.3), custom_call_target="tpu_custom_call" | custom-call | bytes 4194304 | tf_op jit(solution)/shard_map/dequant/pallas_call | solution.py:72
  9.1 4.8 %collective-permute-start = (bf16[64,1024]{1,0:T(8,128)(2,1)}, bf16[64,1024]{1,0:T(8,128)(2,1)S(1)}, u32[]{:S(2)}, u32[]{:S(2)}) collective-permute-start(bf16[64,1024]{1,0:T(8,128)(2,1)} %dequant.1.refs_1_), channel_id=1, source_target_pairs={{0,4},{4,0},{1,5},{5,1},{2,6},{6,2},{3,7},{7,3},{8,12},{12,8},{9,1... | collective-permute-start | bytes 393224 | tf_op jit(solution)/shard_map/dequant/ppermute | solution.py:285
  14.0 3.3 %gradients.2 = (bf16[256,64]{1,0:T(8,128)(2,1)}, f32[64,8,128]{2,1,0:T(8,128)}, f32[64,8,128]{2,1,0:T(8,128)}, s32[1]{0:T(128)}) custom-call(s32[1]{0:T(128)} %bitcast.refs_0_.core, bf16[256,2048]{1,0:T(8,128)(2,1)} %refs_1_.6, bf16[256,1024]{1,0:T(8,128)(2,1)} %refs_1_.7, f32[64,1024]{1,0:T(8,128)} %refs_2_.5), custom_call_target="tpu_custom_call" | custom-call | bytes 4194304 | tf_op jit(solution)/shard_map/gradients/pallas_call | solution.py:72
  17.3 0.9 copy-done.5
  18.2 1.5 %weight_gather.1 = bf16[128,1024]{1,0:T(8,128)(2,1)} custom-call(s32[1]{0:T(128)} %bitcast.1.refs_0_, bf16[64,1024]{1,0:T(8,128)(2,1)S(1)} %copy-done.5, bf16[64,1024]{1,0:T(8,128)(2,1)S(1)} %collective-permute-done.refs_2_, s32[1]{0:T(128)} %get-tuple-element.18.refs_3_), custom_call_target="tpu_custom_call" | custom-call | bytes 4194304 | tf_op jit(solution)/shard_map/weight_gather/pallas_call | solution.py:72
  19.7 7.7 %collective-permute-start.1 = (f32[64,8,128]{2,1,0:T(8,128)}, f32[64,8,128]{2,1,0:T(8,128)S(1)}, u32[]{:S(2)}, u32[]{:S(2)}) collective-permute-start(f32[64,8,128]{2,1,0:T(8,128)} %get-tuple-element.20), channel_id=1, source_target_pairs={{0,64},{64,0},{1,65},{65,1},{2,66},{66,2},{3,67},{67,3},{4,68},{68... | collective-permute-start | bytes 786440 | tf_op jit(solution)/shard_map/gradients/ppermute | solution.py:295
  27.4 3.4 %gradients.3.refs_1_ = f32[64,8,128]{2,1,0:T(8,128)} custom-call(bf16[256,2048]{1,0:T(8,128)(2,1)} %refs_1_.6, bf16[256,1024]{1,0:T(8,128)(2,1)} %refs_1_.7, f32[64,2048]{1,0:T(8,128)} %bitcast.7), custom_call_target="tpu_custom_call" | custom-call | bytes 4194304 | tf_op jit(solution)/shard_map/gradients/pallas_call | solution.py:72
  30.9 0.9 copy-done.4
  31.8 25.7 %all_to_all.20.refs_0_ = bf16[64,16,128]{2,1,0:T(8,128)(2,1)S(1)} all-to-all(bf16[64,16,128]{2,1,0:T(8,128)(2,1)S(1)} %plane_sum.2), channel_id=1, replica_groups=mesh['zh'=4,'c'=2,'y'=8,'zl'=2,'x'=4] {'zh','y','zl'}, dimensions={0} | all-to-all | bytes 524288 | tf_op jit(solution)/shard_map/plane_sum/all_to_all | solution.py:313
  57.6 20.0 %all_to_all.21.gathered = bf16[64,16,128]{2,1,0:T(8,128)(2,1)S(1)} all-to-all(bf16[64,16,128]{2,1,0:T(8,128)(2,1)S(1)} %plane_sum.3), channel_id=1, replica_groups=mesh['zh'=4,'c'=2,'y'=8,'zl'=2,'x'=4] {'zh','y','zl'}, dimensions={0} | all-to-all | bytes 524288 | tf_op jit(solution)/shard_map/plane_sum/all_to_all | solution.py:315
  77.6 0.9 refresh.4
  78.6 4.5 %collective-permute-start.2 = (bf16[1024,1024]{1,0:T(8,128)(2,1)}, bf16[1024,1024]{1,0:T(8,128)(2,1)}, u32[]{:S(2)}, u32[]{:S(2)}) collective-permute-start(bf16[1024,1024]{1,0:T(8,128)(2,1)} %get-tuple-element.21.refs_2_.refs_4_), channel_id=1, source_target_pairs={{0,64},{64,0},{1,65},{65,1},{2,66},{66,2},{3,67},{67,3},{4,68},{68... | collective-permute-start | bytes 6291464 | tf_op jit(solution)/shard_map/values/ppermute | solution.py:320
  83.1 4.1 %all-to-all-start.3 = ((bf16[4,80,1024]{2,1,0:T(8,128)(2,1)}), bf16[4,80,1024]{2,1,0:T(8,128)(2,1)S(1)}, u32[]{:S(2)}, u32[]{:S(2)}) async-start(bf16[4,80,1024]{2,1,0:T(8,128)(2,1)} %get-tuple-element.27), calls=%async_computation.3 | async-start | bytes 1310720 | tf_op jit(solution)/shard_map/refresh/all_to_all | solution.py:318
  87.2 4.9 %values.2 = (bf16[4,256,256]{2,1,0:T(8,128)(2,1)}, s32[1]{0:T(128)}) custom-call(s32[1]{0:T(128)} %bitcast.refs_0_.core, bf16[256,2048]{1,0:T(8,128)(2,1)S(1)} %copy-done.1, bf16[1024,1024]{1,0:T(8,128)(2,1)} %get-tuple-element.21.refs_2_.refs_4_, bf16[1024,1024]{1,0:T(8,128)(2,1)} %collective-permute-done.2.refs_3_.refs_5_, f32[64,2048]{1,0:T(8,128)S(1)} %bitcast.9, ...), custom_call_target="tpu_custom_call" | custom-call | bytes 4194304 | tf_op jit(solution)/shard_map/values/pallas_call | solution.py:72
  92.2 5.3 %grad_tokens.1 = (bf16[256,2048]{1,0:T(8,128)(2,1)}, s32[1]{0:T(128)}) custom-call(s32[1]{0:T(128)} %bitcast.refs_0_.core, bf16[256,1024]{1,0:T(8,128)(2,1)S(1)} %copy-done.2, bf16[256,64]{1,0:T(8,128)(2,1)S(1)} %copy-done.7, f32[64,2048]{1,0:T(8,128)S(1)} %bitcast.10, bf16[1024,1024]{1,0:T(8,128)(2,1)} %get-tuple-element.21.refs_2_.refs_4_, ...), custom_call_target="tpu_custom_call" | custom-call | bytes 4194304 | tf_op jit(solution)/shard_map/grad_tokens/pallas_call | solution.py:72
  97.9 0.7 refresh.6.refs_3_
  98.6 3.0 %collective-permute-start.4 = (bf16[4,80,1024]{2,1,0:T(8,128)(2,1)S(1)}, bf16[4,80,1024]{2,1,0:T(8,128)(2,1)S(1)}, u32[]{:S(2)}, u32[]{:S(2)}) collective-permute-start(bf16[4,80,1024]{2,1,0:T(8,128)(2,1)S(1)} %refresh.6.refs_3_), channel_id=1, source_target_pairs={{0,64},{64,0},{1,65},{65,1},{2,66},{66,2},{3,67},{67,3},{4,68},{68... | collective-permute-start | bytes 1966088 | tf_op jit(solution)/shard_map/refresh/ppermute | solution.py:345
  101.6 3.5 %all-to-all-start.2 = ((bf16[4,256,256]{2,1,0:T(8,128)(2,1)}), bf16[4,256,256]{2,1,0:T(8,128)(2,1)S(1)}, u32[]{:S(2)}, u32[]{:S(2)}) async-start(bf16[4,256,256]{2,1,0:T(8,128)(2,1)} %get-tuple-element.22), calls=%async_computation.2 | async-start | bytes 1048576 | tf_op jit(solution)/shard_map/values/all_to_all | solution.py:328
  105.1 2.0 %collective-permute-start.3 = (bf16[64,1024]{1,0:T(8,128)(2,1)S(1)}, bf16[64,1024]{1,0:T(8,128)(2,1)S(1)}, u32[]{:S(2)}, u32[]{:S(2)}) collective-permute-start(bf16[64,1024]{1,0:T(8,128)(2,1)S(1)} %get-tuple-element.26.refs_2_), channel_id=1, source_target_pairs={{0,64},{64,0},{1,65},{65,1},{2,66},{66,2},{3,67},{67,3},{4,68},{68... | collective-permute-start | bytes 393224 | tf_op jit(solution)/shard_map/refresh/ppermute | solution.py:340
  107.2 1.2 collective-permute-done.3.refs_3_
  108.4 1.5 %refresh.5 = f32[64,2048]{1,0:T(8,128)} custom-call(s32[1]{0:T(128)} %bitcast.refs_0_.core, f32[64,2048]{1,0:T(8,128)S(1)} %bitcast.11, bf16[64,1024]{1,0:T(8,128)(2,1)S(1)} %get-tuple-element.26.refs_2_, bf16[64,1024]{1,0:T(8,128)(2,1)S(1)} %collective-permute-done.3.refs_3_, s32[1]{0:T(128)} %get-tuple-element.24.refs_6_.refs_4_), custom_call_target="tpu_custom_call" | custom-call | bytes 4194304 | tf_op jit(solution)/shard_map/refresh/pallas_call | solution.py:72
  109.9 4.6 %all-to-all-done.2.refs_0_ = bf16[4,256,256]{2,1,0:T(8,128)(2,1)S(1)} async-done(((bf16[4,256,256]{2,1,0:T(8,128)(2,1)}), bf16[4,256,256]{2,1,0:T(8,128)(2,1)S(1)}, u32[]{:S(2)}, u32[]{:S(2)}) %all-to-all-start.2) | async-done | bytes 524320 | tf_op jit(solution)/shard_map/values/all_to_all | solution.py:328
  114.5 0.8 values.3
  115.3 1.1 refresh.7
  (24 shorter events, 0.6 us)
Async XLA Ops:
  7.2 70.4 %all-gather.2.cloned.1.call-start = ((), (), s32[]{:S(2)}) async-start(), calls=%async_computation.4 | async-start | bytes 2359296 | tf_op jit(solution)/shard_map/weight_gather/all_gather | solution.py:308
  9.1 8.1 %collective-permute-start = (bf16[64,1024]{1,0:T(8,128)(2,1)}, bf16[64,1024]{1,0:T(8,128)(2,1)S(1)}, u32[]{:S(2)}, u32[]{:S(2)}) collective-permute-start(bf16[64,1024]{1,0:T(8,128)(2,1)} %dequant.1.refs_1_), channel_id=1, source_target_pairs={{0,4},{4,0},{1,5},{5,1},{2,6},{6,2},{3,7},{7,3},{8,12},{12,8},{9,1... | collective-permute-start | bytes 393224 | tf_op jit(solution)/shard_map/dequant/ppermute | solution.py:285
  17.3 0.9 copy-start.5
  18.2 12.7 %copy-start.6 = (f32[64,8,128]{2,1,0:T(8,128)S(1)}, f32[64,8,128]{2,1,0:T(8,128)}, u32[]{:S(2)}) copy-start(f32[64,8,128]{2,1,0:T(8,128)} %get-tuple-element.19.refs_0_) | copy-start | bytes 786436
  19.7 11.2 %collective-permute-start.1 = (f32[64,8,128]{2,1,0:T(8,128)}, f32[64,8,128]{2,1,0:T(8,128)S(1)}, u32[]{:S(2)}, u32[]{:S(2)}) collective-permute-start(f32[64,8,128]{2,1,0:T(8,128)} %get-tuple-element.20), channel_id=1, source_target_pairs={{0,64},{64,0},{1,65},{65,1},{2,66},{66,2},{3,67},{67,3},{4,68},{68... | collective-permute-start | bytes 786440 | tf_op jit(solution)/shard_map/gradients/ppermute | solution.py:295
  27.4 50.2 %copy-start = (f32[2048,64]{0,1:T(8,128)S(1)}, f32[2048,64]{0,1:T(8,128)}, u32[]{:S(2)}) copy-start(f32[2048,64]{0,1:T(8,128)} %param.10) | copy-start | bytes 1572868
  30.9 1.0 copy-start.4
  77.6 9.6 %copy-start.1 = (bf16[256,2048]{1,0:T(8,128)(2,1)S(1)}, bf16[256,2048]{1,0:T(8,128)(2,1)}, u32[]{:S(2)}) copy-start(bf16[256,2048]{1,0:T(8,128)(2,1)} %refs_1_.6) | copy-start | bytes 3145732
  77.6 9.6 %copy-start.3 = (f32[64,1024]{1,0:T(8,128)S(1)}, f32[64,1024]{1,0:T(8,128)}, u32[]{:S(2)}) copy-start(f32[64,1024]{1,0:T(8,128)} %refs_2_.5) | copy-start | bytes 786436
  78.6 8.6 %collective-permute-start.2 = (bf16[1024,1024]{1,0:T(8,128)(2,1)}, bf16[1024,1024]{1,0:T(8,128)(2,1)}, u32[]{:S(2)}, u32[]{:S(2)}) collective-permute-start(bf16[1024,1024]{1,0:T(8,128)(2,1)} %get-tuple-element.21.refs_2_.refs_4_), channel_id=1, source_target_pairs={{0,64},{64,0},{1,65},{65,1},{2,66},{66,2},{3,67},{67,3},{4,68},{68... | collective-permute-start | bytes 6291464 | tf_op jit(solution)/shard_map/values/ppermute | solution.py:320
  83.1 14.8 %all-to-all-start.3 = ((bf16[4,80,1024]{2,1,0:T(8,128)(2,1)}), bf16[4,80,1024]{2,1,0:T(8,128)(2,1)S(1)}, u32[]{:S(2)}, u32[]{:S(2)}) async-start(bf16[4,80,1024]{2,1,0:T(8,128)(2,1)} %get-tuple-element.27), calls=%async_computation.3 | async-start | bytes 1310720 | tf_op jit(solution)/shard_map/refresh/all_to_all | solution.py:318
  87.2 5.0 %copy-start.2 = (bf16[256,1024]{1,0:T(8,128)(2,1)S(1)}, bf16[256,1024]{1,0:T(8,128)(2,1)}, u32[]{:S(2)}) copy-start(bf16[256,1024]{1,0:T(8,128)(2,1)} %refs_1_.7) | copy-start | bytes 1572868
  87.2 5.0 %copy-start.7 = (bf16[256,64]{1,0:T(8,128)(2,1)S(1)}, bf16[256,64]{1,0:T(8,128)(2,1)}, u32[]{:S(2)}) copy-start(bf16[256,64]{1,0:T(8,128)(2,1)} %get-tuple-element.23.refs_2_) | copy-start | bytes 98308
  98.6 16.7 %collective-permute-start.4 = (bf16[4,80,1024]{2,1,0:T(8,128)(2,1)S(1)}, bf16[4,80,1024]{2,1,0:T(8,128)(2,1)S(1)}, u32[]{:S(2)}, u32[]{:S(2)}) collective-permute-start(bf16[4,80,1024]{2,1,0:T(8,128)(2,1)S(1)} %refresh.6.refs_3_), channel_id=1, source_target_pairs={{0,64},{64,0},{1,65},{65,1},{2,66},{66,2},{3,67},{67,3},{4,68},{68... | collective-permute-start | bytes 1966088 | tf_op jit(solution)/shard_map/refresh/ppermute | solution.py:345
  101.6 12.9 %all-to-all-start.2 = ((bf16[4,256,256]{2,1,0:T(8,128)(2,1)}), bf16[4,256,256]{2,1,0:T(8,128)(2,1)S(1)}, u32[]{:S(2)}, u32[]{:S(2)}) async-start(bf16[4,256,256]{2,1,0:T(8,128)(2,1)} %get-tuple-element.22), calls=%async_computation.2 | async-start | bytes 1048576 | tf_op jit(solution)/shard_map/values/all_to_all | solution.py:328
  105.1 3.2 %collective-permute-start.3 = (bf16[64,1024]{1,0:T(8,128)(2,1)S(1)}, bf16[64,1024]{1,0:T(8,128)(2,1)S(1)}, u32[]{:S(2)}, u32[]{:S(2)}) collective-permute-start(bf16[64,1024]{1,0:T(8,128)(2,1)S(1)} %get-tuple-element.26.refs_2_), channel_id=1, source_target_pairs={{0,64},{64,0},{1,65},{65,1},{2,66},{66,2},{3,67},{67,3},{4,68},{68... | collective-permute-start | bytes 393224 | tf_op jit(solution)/shard_map/refresh/ppermute | solution.py:340
Sparse Core Ops, SparseCore 0:
  19.8 52.4 all-gather.1

commit v6 on v5

--- a/solution.py
+++ b/solution.py
@@ -341,7 +341,7 @@
         refreshed_down = call(
             down_kernel, shape(64, 2048), (core,), (), (down, raw, raw_other), after=(whole,)
         ).T
-        rows = call(copy_kernel, shape(*rows.shape, dtype=bf16), (), (), (rows,), after=(turned,))
+        rows = call(copy_kernel, shape(*rows.shape, dtype=bf16), (), (), (rows,), after=(whole,))
         rows_other = lax.ppermute(rows, "c", swap)
         scorer_a, refreshed_up = call(
             finish_kernel,

time: 124 us -> 124 us (level)
    all_to_all x1, waiting for transfers between devices: 0.38 us -> 5.82 us  [body(): rows = lax.all_to_all(rows, 'x', 0, 0, tiled=True)]
    all_to_all x1, waiting for transfers between devices: 4.64 us -> 0.75 us  [body(): came = lax.all_to_all(sent, 'x', 0, 0, tiled=True)]
    unnamed x16 -> x18, local copies, waits for them, and re-layouts: 1.87 us -> 2.66 us
  transfers between devices with their start and end apart: 8 -> 8, of which waited for: 3 -> 2; matrix products, arithmetic and copies ran while one was open for 0% -> 0% of each run, Pallas kernels for 16% -> 15%
where the time goes in v6:
time: 124 us; the launch traced here: 123 us
  blocking collectives  45.7 us (37%)
  starting transfers between devices  29.6 us (24%)
  Pallas kernels  24.5 us (20%)
  between operations  14.2 us (11%)
  waiting for transfers between devices  6.6 us (5%)
  local copies, waits for them, and re-layouts  2.66 us (2%)
    all_to_all x1, blocking collectives, body(): parts = lax.all_to_all(parts, PLANE, 0, 0, tiled=True)  25.7 us
    pallas_call x12, Pallas kernels, call(): pl.pallas_call(loaded, out_shape=outs, in_specs=[pl.BlockSpec(memory_spac...  23.6 us
    all_to_all x1, blocking collectives, body(): gathered = lax.all_to_all(total, PLANE, 0, 0, tiled=True)  20 us
    ppermute x1, starting transfers between devices, body(): arrived = lax.ppermute(send, 'c', swap)  7.7 us
    all_to_all x1, waiting for transfers between devices, body(): rows = lax.all_to_all(rows, 'x', 0, 0, tiled=True)  5.82 us
    ppermute x1, starting transfers between devices, body(): theirs = lax.ppermute(mine, 'zl', swap)  4.83 us
    ppermute x1, starting transfers between devices, body(): far = lax.ppermute(near, 'c', swap)  4.52 us
    all_to_all x1, starting transfers between devices, body(): rows = lax.all_to_all(rows, 'x', 0, 0, tiled=True)  4.1 us
  transfers between devices with their start and end apart: 8, of which 2 were waited for; matrix products, arithmetic and copies ran while one was open for 0% of the time, Pallas kernels for 15%

profile of v6, /device:TPU:1, one launch (start us, length us, event | category | flops | bytes accessed | tf_op | source)
XLA Modules:
  0.0 123.3 jit_solution(10791540952057777022)
XLA Ops:
  7.2 1.9 %dequant.1.refs_1_ = bf16[64,1024]{1,0:T(8,128)(2,1)} custom-call(s32[1]{0:T(128)} %bitcast.refs_0_.core, bf16[64,2048]{1,0:T(8,128)(2,1)} %bitcast.13, bf16[16,64]{1,0:T(8,128)(2,1)} %refs_2_.3), custom_call_target="tpu_custom_call" | custom-call | bytes 4194304 | tf_op jit(solution)/shard_map/dequant/pallas_call | solution.py:72
  9.1 4.8 %collective-permute-start = (bf16[64,1024]{1,0:T(8,128)(2,1)}, bf16[64,1024]{1,0:T(8,128)(2,1)S(1)}, u32[]{:S(2)}, u32[]{:S(2)}) collective-permute-start(bf16[64,1024]{1,0:T(8,128)(2,1)} %dequant.1.refs_1_), channel_id=1, source_target_pairs={{0,4},{4,0},{1,5},{5,1},{2,6},{6,2},{3,7},{7,3},{8,12},{12,8},{9,1... | collective-permute-start | bytes 393224 | tf_op jit(solution)/shard_map/dequant/ppermute | solution.py:285
  14.0 3.3 %gradients.2 = (bf16[256,64]{1,0:T(8,128)(2,1)}, f32[64,8,128]{2,1,0:T(8,128)}, f32[64,8,128]{2,1,0:T(8,128)}, s32[1]{0:T(128)}) custom-call(s32[1]{0:T(128)} %bitcast.refs_0_.core, bf16[256,2048]{1,0:T(8,128)(2,1)} %refs_1_.6, bf16[256,1024]{1,0:T(8,128)(2,1)} %refs_1_.7, f32[64,1024]{1,0:T(8,128)} %refs_2_.5), custom_call_target="tpu_custom_call" | custom-call | bytes 4194304 | tf_op jit(solution)/shard_map/gradients/pallas_call | solution.py:72
  17.3 0.9 copy-done.6
  18.2 1.3 %weight_gather.1 = bf16[128,1024]{1,0:T(8,128)(2,1)} custom-call(s32[1]{0:T(128)} %bitcast.1.refs_0_, bf16[64,1024]{1,0:T(8,128)(2,1)S(1)} %copy-done.6, bf16[64,1024]{1,0:T(8,128)(2,1)S(1)} %collective-permute-done.refs_2_, s32[1]{0:T(128)} %get-tuple-element.17.refs_3_), custom_call_target="tpu_custom_call" | custom-call | bytes 4194304 | tf_op jit(solution)/shard_map/weight_gather/pallas_call | solution.py:72
  19.5 7.7 %collective-permute-start.1 = (f32[64,8,128]{2,1,0:T(8,128)}, f32[64,8,128]{2,1,0:T(8,128)S(1)}, u32[]{:S(2)}, u32[]{:S(2)}) collective-permute-start(f32[64,8,128]{2,1,0:T(8,128)} %get-tuple-element.19), channel_id=1, source_target_pairs={{0,64},{64,0},{1,65},{65,1},{2,66},{66,2},{3,67},{67,3},{4,68},{68... | collective-permute-start | bytes 786440 | tf_op jit(solution)/shard_map/gradients/ppermute | solution.py:295
  27.3 3.4 %gradients.3.refs_1_ = f32[64,8,128]{2,1,0:T(8,128)} custom-call(bf16[256,2048]{1,0:T(8,128)(2,1)} %refs_1_.6, bf16[256,1024]{1,0:T(8,128)(2,1)} %refs_1_.7, f32[64,2048]{1,0:T(8,128)} %bitcast.7), custom_call_target="tpu_custom_call" | custom-call | bytes 4194304 | tf_op jit(solution)/shard_map/gradients/pallas_call | solution.py:72
  30.7 0.9 copy-done.4
  31.7 25.7 %all_to_all.20.refs_0_ = bf16[64,16,128]{2,1,0:T(8,128)(2,1)S(1)} all-to-all(bf16[64,16,128]{2,1,0:T(8,128)(2,1)S(1)} %plane_sum.2), channel_id=1, replica_groups=mesh['zh'=4,'c'=2,'y'=8,'zl'=2,'x'=4] {'zh','y','zl'}, dimensions={0} | all-to-all | bytes 524288 | tf_op jit(solution)/shard_map/plane_sum/all_to_all | solution.py:313
  57.5 20.0 %all_to_all.21.gathered = bf16[64,16,128]{2,1,0:T(8,128)(2,1)S(1)} all-to-all(bf16[64,16,128]{2,1,0:T(8,128)(2,1)S(1)} %plane_sum.3), channel_id=1, replica_groups=mesh['zh'=4,'c'=2,'y'=8,'zl'=2,'x'=4] {'zh','y','zl'}, dimensions={0} | all-to-all | bytes 524288 | tf_op jit(solution)/shard_map/plane_sum/all_to_all | solution.py:315
  77.5 0.9 refresh.4
  78.4 4.5 %collective-permute-start.2 = (bf16[1024,1024]{1,0:T(8,128)(2,1)}, bf16[1024,1024]{1,0:T(8,128)(2,1)}, u32[]{:S(2)}, u32[]{:S(2)}) collective-permute-start(bf16[1024,1024]{1,0:T(8,128)(2,1)} %get-tuple-element.20.refs_2_.refs_4_), channel_id=1, source_target_pairs={{0,64},{64,0},{1,65},{65,1},{2,66},{66,2},{3,67},{67,3},{4,68},{68... | collective-permute-start | bytes 6291464 | tf_op jit(solution)/shard_map/values/ppermute | solution.py:320
  83.0 4.1 %all-to-all-start.3 = ((bf16[4,80,1024]{2,1,0:T(8,128)(2,1)}), bf16[4,80,1024]{2,1,0:T(8,128)(2,1)S(1)}, u32[]{:S(2)}, u32[]{:S(2)}) async-start(bf16[4,80,1024]{2,1,0:T(8,128)(2,1)} %get-tuple-element.26), calls=%async_computation.3 | async-start | bytes 1310720 | tf_op jit(solution)/shard_map/refresh/all_to_all | solution.py:318
  87.1 4.1 %values.2 = (bf16[4,256,256]{2,1,0:T(8,128)(2,1)S(1)}, s32[1]{0:T(128)}) custom-call(s32[1]{0:T(128)} %bitcast.refs_0_.core, bf16[256,2048]{1,0:T(8,128)(2,1)S(1)} %copy-done.1, bf16[1024,1024]{1,0:T(8,128)(2,1)} %get-tuple-element.20.refs_2_.refs_4_, bf16[1024,1024]{1,0:T(8,128)(2,1)} %collective-permute-done.2.refs_3_.refs_5_, f32[64,2048]{1,0:T(8,128)S(1)} %bitcast.9, ...), custom_call_target="tpu_custom_call" | custom-call | bytes 4194304 | tf_op jit(solution)/shard_map/values/pallas_call | solution.py:72
  91.2 0.8 copy-done.5
  92.0 5.8 %all-to-all-done.3.refs_0_ = bf16[4,80,1024]{2,1,0:T(8,128)(2,1)S(1)} async-done(((bf16[4,80,1024]{2,1,0:T(8,128)(2,1)}), bf16[4,80,1024]{2,1,0:T(8,128)(2,1)S(1)}, u32[]{:S(2)}, u32[]{:S(2)}) %all-to-all-start.3) | async-done | bytes 655392 | tf_op jit(solution)/shard_map/refresh/all_to_all | solution.py:318
  98.5 3.0 %collective-permute-start.4 = (bf16[4,80,1024]{2,1,0:T(8,128)(2,1)S(1)}, bf16[4,80,1024]{2,1,0:T(8,128)(2,1)S(1)}, u32[]{:S(2)}, u32[]{:S(2)}) collective-permute-start(bf16[4,80,1024]{2,1,0:T(8,128)(2,1)S(1)} %refresh.6.refs_3_), channel_id=1, source_target_pairs={{0,64},{64,0},{1,65},{65,1},{2,66},{66,2},{3,67},{67,3},{4,68},{68... | collective-permute-start | bytes 1966088 | tf_op jit(solution)/shard_map/refresh/ppermute | solution.py:345
  101.5 3.5 %all-to-all-start.2 = ((bf16[4,256,256]{2,1,0:T(8,128)(2,1)}), bf16[4,256,256]{2,1,0:T(8,128)(2,1)S(1)}, u32[]{:S(2)}, u32[]{:S(2)}) async-start(bf16[4,256,256]{2,1,0:T(8,128)(2,1)} %copy-done.5), calls=%async_computation.2 | async-start | bytes 1048576 | tf_op jit(solution)/shard_map/values/all_to_all | solution.py:328
  105.0 1.9 %collective-permute-start.3 = (bf16[64,1024]{1,0:T(8,128)(2,1)S(1)}, bf16[64,1024]{1,0:T(8,128)(2,1)S(1)}, u32[]{:S(2)}, u32[]{:S(2)}) collective-permute-start(bf16[64,1024]{1,0:T(8,128)(2,1)S(1)} %get-tuple-element.25.refs_2_), channel_id=1, source_target_pairs={{0,64},{64,0},{1,65},{65,1},{2,66},{66,2},{3,67},{67,3},{4,68},{68... | collective-permute-start | bytes 393224 | tf_op jit(solution)/shard_map/refresh/ppermute | solution.py:340
  107.0 5.3 %grad_tokens.1 = (bf16[256,2048]{1,0:T(8,128)(2,1)}, s32[1]{0:T(128)}) custom-call(s32[1]{0:T(128)} %bitcast.refs_0_.core, bf16[256,1024]{1,0:T(8,128)(2,1)S(1)} %copy-done.2, bf16[256,64]{1,0:T(8,128)(2,1)S(1)} %copy-done.8, f32[64,2048]{1,0:T(8,128)S(1)} %bitcast.10, bf16[1024,1024]{1,0:T(8,128)(2,1)} %get-tuple-element.20.refs_2_.refs_4_, ...), custom_call_target="tpu_custom_call" | custom-call | bytes 4194304 | tf_op jit(solution)/shard_map/grad_tokens/pallas_call | solution.py:72
  112.3 1.5 %refresh.5 = f32[64,2048]{1,0:T(8,128)} custom-call(s32[1]{0:T(128)} %bitcast.refs_0_.core, f32[64,2048]{1,0:T(8,128)S(1)} %bitcast.11, bf16[64,1024]{1,0:T(8,128)(2,1)S(1)} %get-tuple-element.25.refs_2_, bf16[64,1024]{1,0:T(8,128)(2,1)S(1)} %collective-permute-done.3.refs_3_, s32[1]{0:T(128)} %get-tuple-element.23.refs_6_.refs_4_.refs_1_), custom_call_target="tpu_custom_call" | custom-call | bytes 4194304 | tf_op jit(solution)/shard_map/refresh/pallas_call | solution.py:72
  113.9 0.8 all-to-all-done.2.refs_0_
  114.6 0.8 values.3
  115.4 1.1 refresh.7
  (26 shorter events, 0.9 us)
Async XLA Ops:
  7.2 70.3 %all-gather.2.cloned.1.call-start = ((), (), s32[]{:S(2)}) async-start(), calls=%async_computation.4 | async-start | bytes 2359296 | tf_op jit(solution)/shard_map/weight_gather/all_gather | solution.py:308
  9.1 8.1 %collective-permute-start = (bf16[64,1024]{1,0:T(8,128)(2,1)}, bf16[64,1024]{1,0:T(8,128)(2,1)S(1)}, u32[]{:S(2)}, u32[]{:S(2)}) collective-permute-start(bf16[64,1024]{1,0:T(8,128)(2,1)} %dequant.1.refs_1_), channel_id=1, source_target_pairs={{0,4},{4,0},{1,5},{5,1},{2,6},{6,2},{3,7},{7,3},{8,12},{12,8},{9,1... | collective-permute-start | bytes 393224 | tf_op jit(solution)/shard_map/dequant/ppermute | solution.py:285
  17.3 0.9 copy-start.6
  18.2 12.5 %copy-start.7 = (f32[64,8,128]{2,1,0:T(8,128)S(1)}, f32[64,8,128]{2,1,0:T(8,128)}, u32[]{:S(2)}) copy-start(f32[64,8,128]{2,1,0:T(8,128)} %get-tuple-element.18.refs_0_) | copy-start | bytes 786436
  19.5 11.2 %collective-permute-start.1 = (f32[64,8,128]{2,1,0:T(8,128)}, f32[64,8,128]{2,1,0:T(8,128)S(1)}, u32[]{:S(2)}, u32[]{:S(2)}) collective-permute-start(f32[64,8,128]{2,1,0:T(8,128)} %get-tuple-element.19), channel_id=1, source_target_pairs={{0,64},{64,0},{1,65},{65,1},{2,66},{66,2},{3,67},{67,3},{4,68},{68... | collective-permute-start | bytes 786440 | tf_op jit(solution)/shard_map/gradients/ppermute | solution.py:295
  27.3 50.2 %copy-start = (f32[2048,64]{0,1:T(8,128)S(1)}, f32[2048,64]{0,1:T(8,128)}, u32[]{:S(2)}) copy-start(f32[2048,64]{0,1:T(8,128)} %param.10) | copy-start | bytes 1572868
  30.7 1.0 copy-start.4
  77.5 9.6 %copy-start.1 = (bf16[256,2048]{1,0:T(8,128)(2,1)S(1)}, bf16[256,2048]{1,0:T(8,128)(2,1)}, u32[]{:S(2)}) copy-start(bf16[256,2048]{1,0:T(8,128)(2,1)} %refs_1_.6) | copy-start | bytes 3145732
  77.5 9.6 %copy-start.3 = (f32[64,1024]{1,0:T(8,128)S(1)}, f32[64,1024]{1,0:T(8,128)}, u32[]{:S(2)}) copy-start(f32[64,1024]{1,0:T(8,128)} %refs_2_.5) | copy-start | bytes 786436
  78.4 8.6 %collective-permute-start.2 = (bf16[1024,1024]{1,0:T(8,128)(2,1)}, bf16[1024,1024]{1,0:T(8,128)(2,1)}, u32[]{:S(2)}, u32[]{:S(2)}) collective-permute-start(bf16[1024,1024]{1,0:T(8,128)(2,1)} %get-tuple-element.20.refs_2_.refs_4_), channel_id=1, source_target_pairs={{0,64},{64,0},{1,65},{65,1},{2,66},{66,2},{3,67},{67,3},{4,68},{68... | collective-permute-start | bytes 6291464 | tf_op jit(solution)/shard_map/values/ppermute | solution.py:320
  83.0 14.8 %all-to-all-start.3 = ((bf16[4,80,1024]{2,1,0:T(8,128)(2,1)}), bf16[4,80,1024]{2,1,0:T(8,128)(2,1)S(1)}, u32[]{:S(2)}, u32[]{:S(2)}) async-start(bf16[4,80,1024]{2,1,0:T(8,128)(2,1)} %get-tuple-element.26), calls=%async_computation.3 | async-start | bytes 1310720 | tf_op jit(solution)/shard_map/refresh/all_to_all | solution.py:318
  91.2 0.8 copy-start.5
  92.0 15.0 %copy-start.2 = (bf16[256,1024]{1,0:T(8,128)(2,1)S(1)}, bf16[256,1024]{1,0:T(8,128)(2,1)}, u32[]{:S(2)}) copy-start(bf16[256,1024]{1,0:T(8,128)(2,1)} %refs_1_.7) | copy-start | bytes 1572868
  92.0 15.0 %copy-start.8 = (bf16[256,64]{1,0:T(8,128)(2,1)S(1)}, bf16[256,64]{1,0:T(8,128)(2,1)}, u32[]{:S(2)}) copy-start(bf16[256,64]{1,0:T(8,128)(2,1)} %get-tuple-element.22.refs_2_) | copy-start | bytes 98308
  98.5 16.9 %collective-permute-start.4 = (bf16[4,80,1024]{2,1,0:T(8,128)(2,1)S(1)}, bf16[4,80,1024]{2,1,0:T(8,128)(2,1)S(1)}, u32[]{:S(2)}, u32[]{:S(2)}) collective-permute-start(bf16[4,80,1024]{2,1,0:T(8,128)(2,1)S(1)} %refresh.6.refs_3_), channel_id=1, source_target_pairs={{0,64},{64,0},{1,65},{65,1},{2,66},{66,2},{3,67},{67,3},{4,68},{68... | collective-permute-start | bytes 1966088 | tf_op jit(solution)/shard_map/refresh/ppermute | solution.py:345
  101.5 13.1 %all-to-all-start.2 = ((bf16[4,256,256]{2,1,0:T(8,128)(2,1)}), bf16[4,256,256]{2,1,0:T(8,128)(2,1)S(1)}, u32[]{:S(2)}, u32[]{:S(2)}) async-start(bf16[4,256,256]{2,1,0:T(8,128)(2,1)} %copy-done.5), calls=%async_computation.2 | async-start | bytes 1048576 | tf_op jit(solution)/shard_map/values/all_to_all | solution.py:328
  105.0 7.3 %collective-permute-start.3 = (bf16[64,1024]{1,0:T(8,128)(2,1)S(1)}, bf16[64,1024]{1,0:T(8,128)(2,1)S(1)}, u32[]{:S(2)}, u32[]{:S(2)}) collective-permute-start(bf16[64,1024]{1,0:T(8,128)(2,1)S(1)} %get-tuple-element.25.refs_2_), channel_id=1, source_target_pairs={{0,64},{64,0},{1,65},{65,1},{2,66},{66,2},{3,67},{67,3},{4,68},{68... | collective-permute-start | bytes 393224 | tf_op jit(solution)/shard_map/refresh/ppermute | solution.py:340
Sparse Core Ops, SparseCore 0:
  19.7 52.6 all-gather.1
